TPU v7x, 128 devices: a whole 4x4x4 slice. The times are simulated.
128 devices in a mesh: seq: 8 (over z, core), dp: 16 (over y, x).
Axes of the slice: x: 4, y: 4, z: 4, core: 2. Of those that a mesh axis runs over, the one named last changes fastest.
Arguments:
- inputs: bfloat16 [16, 1024, 768], P('dp', 'seq'), may hold values from -6 to 6
- doc_ids: int32 [16, 1024], P('dp', 'seq'), may hold values from 0 to 4, as said below
- cotangent: bfloat16 [16, 1024, 768], P('dp', 'seq'), may hold values from -6 to 6
- w_query: float32 [768, 768], P(('seq', 'dp')), may hold values from -0.21875 to 0.21875
- w_key: float32 [768, 768], P(('seq', 'dp')), may hold values from -0.21875 to 0.21875
- w_value: float32 [768, 768], P(('seq', 'dp')), may hold values from -0.21875 to 0.21875
- w_output: float32 [768, 768], P(('seq', 'dp')), may hold values from -3.5 to 3.5
- w_gate: float32 [768, 3072], P(('seq', 'dp')), may hold values from -0.21875 to 0.21875
- w_up: float32 [768, 3072], P(('seq', 'dp')), may hold values from -0.21875 to 0.21875
- w_down: float32 [3072, 768], P(('seq', 'dp')), may hold values from -0.109375 to 0.109375
- norm_gains: float32 [768, 2], P(('seq', 'dp')), may hold values from 0.5 to 1.5
- mom_query: float32 [768, 768], P(('seq', 'dp')), may hold values from -80 to 80
- mom_key: float32 [768, 768], P(('seq', 'dp')), may hold values from -80 to 80
- mom_value: float32 [768, 768], P(('seq', 'dp')), may hold values from -80 to 80
- mom_output: float32 [768, 768], P(('seq', 'dp')), may hold values from -3.5 to 3.5
- mom_gate: float32 [768, 3072], P(('seq', 'dp')), may hold values from -40 to 40
- mom_up: float32 [768, 3072], P(('seq', 'dp')), may hold values from -40 to 40
- mom_down: float32 [3072, 768], P(('seq', 'dp')), may hold values from -40 to 40
- mom_gains: float32 [768, 2], P(('seq', 'dp')), may hold values from -80 to 80
- avg_query: float32 [768, 768], P(('seq', 'dp')), may hold values from -0.21875 to 0.21875
- avg_key: float32 [768, 768], P(('seq', 'dp')), may hold values from -0.21875 to 0.21875
- avg_value: float32 [768, 768], P(('seq', 'dp')), may hold values from -0.21875 to 0.21875
- avg_output: float32 [768, 768], P(('seq', 'dp')), may hold values from -3.5 to 3.5
- avg_gate: float32 [768, 3072], P(('seq', 'dp')), may hold values from -0.21875 to 0.21875
- avg_up: float32 [768, 3072], P(('seq', 'dp')), may hold values from -0.21875 to 0.21875
- avg_down: float32 [3072, 768], P(('seq', 'dp')), may hold values from -0.109375 to 0.109375
- avg_gains: float32 [768, 2], P(('seq', 'dp')), may hold values from 0.5 to 1.5
Outputs:
- output: bfloat16 [16, 1024, 768], P('dp', 'seq')
- input_grad: float32 [16, 1024, 768], P('dp', 'seq')
- new_query: float32 [768, 768], P(('seq', 'dp'))
- new_key: float32 [768, 768], P(('seq', 'dp'))
- new_value: float32 [768, 768], P(('seq', 'dp'))
- new_output: float32 [768, 768], P(('seq', 'dp'))
- new_gate: float32 [768, 3072], P(('seq', 'dp'))
- new_up: float32 [768, 3072], P(('seq', 'dp'))
- new_down: float32 [3072, 768], P(('seq', 'dp'))
- new_gains: float32 [768, 2], P(('seq', 'dp'))
- moment_query: float32 [768, 768], P(('seq', 'dp'))
- moment_key: float32 [768, 768], P(('seq', 'dp'))
- moment_value: float32 [768, 768], P(('seq', 'dp'))
- moment_output: float32 [768, 768], P(('seq', 'dp'))
- moment_gate: float32 [768, 3072], P(('seq', 'dp'))
- moment_up: float32 [768, 3072], P(('seq', 'dp'))
- moment_down: float32 [3072, 768], P(('seq', 'dp'))
- moment_gains: float32 [768, 2], P(('seq', 'dp'))
- mean_query: float32 [768, 768], P(('seq', 'dp'))
- mean_key: float32 [768, 768], P(('seq', 'dp'))
- mean_value: float32 [768, 768], P(('seq', 'dp'))
- mean_output: float32 [768, 768], P(('seq', 'dp'))
- mean_gate: float32 [768, 3072], P(('seq', 'dp'))
- mean_up: float32 [768, 3072], P(('seq', 'dp'))
- mean_down: float32 [3072, 768], P(('seq', 'dp'))
- mean_gains: float32 [768, 2], P(('seq', 'dp'))
- copy_query: bfloat16 [768, 768], P(('seq', 'dp'))
- copy_key: bfloat16 [768, 768], P(('seq', 'dp'))
- copy_value: bfloat16 [768, 768], P(('seq', 'dp'))
- copy_output: bfloat16 [768, 768], P(('seq', 'dp'))
- copy_gate: bfloat16 [768, 3072], P(('seq', 'dp'))
- copy_up: bfloat16 [768, 3072], P(('seq', 'dp'))
- copy_down: bfloat16 [3072, 768], P(('seq', 'dp'))
- copy_gains: bfloat16 [768, 2], P(('seq', 'dp'))
Inputs may be any that keep to these rules, and one draw needn't show every extreme that they name: `doc_ids`: ids never fall along a sequence and start at 0; in every sequence one document begins within the first device's block of 128 tokens and ends within the last one's.
All inputs are finite; a program needn't handle non-finite values.
Results may differ from a plain program's by a relative error of at most 0.02.
Values may be sent and summed in bfloat16 or wider, within the bound.
No kernel may reach another device: no remote copies, remote signals or barrier semaphores. Data moves between devices by JAX's collectives and lax.ppermute only.
A program may use at most 192 MiB of HBM per device.

v0:
```python
import functools
import math

import jax
import jax.numpy as jnp
import numpy as np
from jax import lax
from jax.experimental import pallas as pl
from jax.experimental.pallas import tpu as pltpu
from jax.sharding import Mesh
from jax.sharding import PartitionSpec as P


BF = jnp.bfloat16
F32 = jnp.float32
HD = 64
D = 768
FF = 3072
HALF = 384
TOK = 256
LEN = 1024
HEADS = 6
EPS = 1e-05
MOMENTUM = 0.9
AVERAGE = 0.5
RATES = (0.01, 0.01, 0.01, 4.0, 0.02, 0.02, 0.015, 0.1)
MASKED = -1e30
AXES = ("z", "core", "y", "x")


def params(mib=60):
    return pltpu.CompilerParams(vmem_limit_bytes=mib * 1024 * 1024)


def cost(micros):
    return pl.CostEstimate(flops=1 + int(micros * 1e3), bytes_accessed=1, transcendentals=0)


def device_pairs(move):
    pairs = []
    for z in range(4):
        for c in range(2):
            for y in range(4):
                for x in range(4):
                    to = move(z, c, y, x)
                    pairs.append((((z * 2 + c) * 4 + y) * 4 + x, ((to[0] * 2 + to[1]) * 4 + to[2]) * 4 + to[3]))
    return pairs


CORE_PAIRS = device_pairs(lambda z, c, y, x: (z, 1 - c, y, x))


AXIS = {"z": 0, "y": 2, "x": 3}
FLIPS = (0, 1, 3, 2)
ORDERS = (("x", "y", "z"), ("y", "z", "x"), ("z", "x", "y"))


def flip_pairs(axis, flip):
    def move(z, c, y, x):
        at = [z, c, y, x]
        at[AXIS[axis]] = (((at[AXIS[axis]] + c) % 4 ^ flip) - c) % 4
        return tuple(at)

    return device_pairs(move)


def permute(value, pairs):
    return lax.ppermute(value, AXES, pairs)


def cube_groups(flip):
    groups = {}
    for z in range(4):
        for c in range(2):
            for y in range(4):
                for x in range(4):
                    u = [(v + c) % 4 for v in (z, y, x)]
                    key = (c,) + tuple(min(v, v ^ flip) for v in u)
                    place = sum((v & 1 if flip == 1 else v >> 1) << (2 - k) for k, v in enumerate(u))
                    groups.setdefault(key, [None] * 8)[place] = ((z * 2 + c) * 4 + y) * 4 + x
    return list(groups.values())


def exchange(blocks, flip):
    return lax.all_to_all(blocks, AXES, 0, 0, tiled=True, axis_index_groups=cube_groups(flip))


def chip_of_place(me, core):
    place = np.arange(64)
    rows = []
    for order in ORDERS + (None,):
        at = {}
        for k, axis in enumerate("zyx"):
            low = jnp.asarray((place >> (2 - k)) & 1)
            high = jnp.asarray((place >> (5 - (order.index(axis) if order else k))) & 1)
            if order:
                high = high ^ (((me[axis] + core) % 4) >> 1)
            at[axis] = (high * 2 + low - core) % 4
        rows.append(at["z"] * 16 + at["y"] * 4 + at["x"])
    return jnp.stack(rows).astype(jnp.int32)


def spread_matrix():
    place = jnp.arange(512, dtype=jnp.int32)
    chip, core, row = place // 16, (place // 8) % 2, place % 8
    wanted = jnp.where(row < 6, ((chip // 16 * 2 + core) * 16 + chip % 16) * 6 + row, -1)
    return (lax.broadcasted_iota(jnp.int32, (HALF, 512), 0) == wanted[None, :]).astype(BF)


def placed_features(chips):
    row = jnp.arange(12, dtype=jnp.int32)[None, None, :]
    chip = chips[:, :, None]
    wanted = (((chip // 16) * 2 + row // 6) * 16 + chip % 16) * 6 + row % 6
    return jnp.pad(wanted.reshape(4, D), ((0, 4), (0, 0)))


def placed_matrix(wanted):
    return (lax.broadcasted_iota(jnp.int32, (D, D), 0) == wanted).astype(BF)


def dot(left, right):
    return jnp.dot(left, right, preferred_element_type=F32)


def dot_nt(left, right):
    return lax.dot_general(left, right, (((1,), (1,)), ((), ())), preferred_element_type=F32)


def dot_tn(left, right):
    return lax.dot_general(left, right, (((0,), (0,)), ((), ())), preferred_element_type=F32)


def swap_halves(tile):
    lane = lax.broadcasted_iota(jnp.int32, tile.shape, 1)
    return jnp.where(lane % HD < HD // 2, pltpu.roll(tile, 96, 1), pltpu.roll(tile, 32, 1))


def lanes_of(tile, odd):
    lane = lax.broadcasted_iota(jnp.int32, tile.shape, 1)
    return jnp.where((lane >= HD) == bool(odd), tile, jnp.zeros_like(tile))


def join_lanes(even, odd):
    lane = lax.broadcasted_iota(jnp.int32, even.shape, 1)
    return jnp.where(lane < HD, even, odd)


def put_halves(core, w, keep, send, at):
    for part in range(w.shape[1] // D):
        halves = [w[:, part * D + h * HALF : part * D + (h + 1) * HALF] for h in range(2)]
        keep[at + part, 0:6, :] = jnp.where(core == 0, halves[0], halves[1])
        send[at + part, 0:6, :] = jnp.where(core == 0, halves[1], halves[0])
        keep[at + part, 6:8, :] = jnp.zeros((2, HALF), F32)
        send[at + part, 6:8, :] = jnp.zeros((2, HALF), F32)


def pack_ffn_kernel(scal, wg, wu, keep, send):
    put_halves(scal[1], wg, keep, send, 0)
    put_halves(scal[1], wu, keep, send, 4)


def pack_attn_kernel(scal, wq, wk, wv, wo, gains, keep, send, lines):
    core = scal[1]
    for k, w in enumerate((wq, wk, wv)):
        put_halves(core, w, keep, send, k)
    for h in range(2):
        for out in (keep, send):
            out[3 + h, 0:6, :] = wo[:, h * HALF : (h + 1) * HALF]
            out[3 + h, 6:8, :] = jnp.zeros((2, HALF), F32)
    lines[...] = jnp.zeros_like(lines)
    lines[0:2, 0:6] = gains[...]
    moved = jnp.where(core == 0, lines[...], pltpu.roll(lines[...], 8, 1))
    keep[0, 6:8, 0:128] = moved[0:2, :]
    send[0, 6:8, 0:128] = moved[0:2, :]


def both_cores(core, keep, other):
    low = jnp.where(core == 0, keep, other)
    high = jnp.where(core == 0, other, keep)
    return jnp.concatenate([low, high], axis=0).astype(BF)


def merge_ffn_kernel(scal, keep, other, wd, ffn):
    for k in range(8):
        ffn[k] = both_cores(scal[1], keep[k], other[k])
    for j in range(3):
        rows = wd[8 * j : 8 * j + 8, :]
        ffn[8 + j] = jnp.concatenate([rows[:, :HALF], rows[:, HALF:]], axis=0).astype(BF)


def merge_attn_kernel(scal, keep, other, attn):
    for k in range(5):
        value = both_cores(scal[1], keep[k], other[k])
        for copy in range(8):
            attn[copy, k] = value


def dense_rows():
    to = lax.broadcasted_iota(jnp.int32, (96, 128), 0)
    at = lax.broadcasted_iota(jnp.int32, (96, 128), 1)
    row = to % 12
    return (at == (to // 12) * 16 + (row // 6) * 8 + row % 6).astype(BF)


def dense_kernel(blocks, attn):
    pick = dense_rows()
    to = lax.broadcasted_iota(jnp.int32, (32, 128), 0)
    at = lax.broadcasted_iota(jnp.int32, (32, 128), 1)
    gains = ((at // 16 == to % 8) & (at % 8 == 6 + to // 8) & (to < 16)).astype(BF)
    rows = [blocks[:, k].reshape(128, HALF) for k in range(5)]
    found = [dot(pick, value).astype(BF) for value in rows] + [dot(gains, rows[0]).astype(BF)]
    for copy in range(8):
        for k, value in enumerate(found):
            attn[copy, 96 * k : 96 * k + value.shape[0], :] = value


def weight_at(attn, k):
    return attn[:, 96 * k : 96 * k + 96, :].reshape(D, HALF)


def attn_forward_kernel(
    scal,
    seq,
    seq_other,
    cosine,
    sine,
    start,
    wanted,
    attn,
    q,
    k_all,
    v_all,
    h_all,
    h_t,
    x_chip,
    probs,
    po,
    g1_out,
    g2_out,
    x_all,
    bias,
    pa,
):
    z, core = scal[0], scal[1]
    own = pl.ds(pl.multiple_of(z * TOK, TOK), TOK)
    pa[...] = placed_matrix(wanted[3:4, :])
    held = attn[:, 480:496, 0:128].astype(F32).reshape(8, 2, 8, 128)
    block = lax.broadcasted_iota(jnp.int32, (64, D), 0)
    place = lax.broadcasted_iota(jnp.int32, (64, D), 1)
    lane = lax.broadcasted_iota(jnp.int32, (128, D), 0)
    row = lax.broadcasted_iota(jnp.int32, (128, D), 1) % 12
    fold = (lane == (row // 6) * 8 + row % 6).astype(BF)
    for k, out in ((0, g1_out), (1, g2_out)):
        wide = dot(held[:, k].reshape(64, 128).astype(BF), fold)
        line = jnp.sum(jnp.where(place // 12 == block, wide, 0.0), axis=0, keepdims=True)
        out[...] = dot_nt(jnp.broadcast_to(line, (8, D)).astype(BF), pa[...])
    g1 = g1_out[0:1, :]
    wq, wk, wv = (weight_at(attn, k) for k in range(3))

    def turn(raw, at, t):
        u = raw[:, 128 * t : 128 * t + 128]
        return (u * cosine[at, :] + swap_halves(u) * sine[at, :]).astype(BF)

    for c, blocks in ((core, seq), (1 - core, seq_other)):
        for k, flip in enumerate(FLIPS):
            at = (((z + c) % 4 ^ flip) + 4 - c) % 4 * TOK + c * 128
            x_all[pl.ds(pl.multiple_of(at, 128), 128), :] = blocks[k, 0:128, :]
    x_chip[...] = x_all[own, :]
    for b in range(4):
        at = slice(b * TOK, (b + 1) * TOK)
        x16 = x_all[at, :]
        x = x16.astype(F32)
        scale = lax.rsqrt(jnp.mean(x * x, axis=1, keepdims=True) + EPS)
        h1 = dot((x * scale * g1).astype(BF), pa[...]).astype(BF)
        h_all[at, :] = h1
        raw = dot(h1, wk)
        for t in range(3):
            k_all[at, 128 * t : 128 * t + 128] = turn(raw, at, t)
        v_all[at, :] = dot(h1, wv).astype(BF)

    raw = dot(h_all[own, :], wq)
    for t in range(3):
        q[:, 128 * t : 128 * t + 128] = turn(raw, own, t) * BF(0.125)

    key = lax.broadcasted_iota(jnp.int32, (LEN, TOK), 0).astype(F32)
    query = (lax.broadcasted_iota(jnp.int32, (LEN, TOK), 1) + z * TOK).astype(F32)
    bias[...] = jnp.where((key >= start[0:1, own]) & (key <= query), 0.0, MASKED)
    sub = lax.broadcasted_iota(jnp.int32, (128, TOK), 0)
    for t in range(3):
        cols = slice(128 * t, 128 * t + 128)
        q_tile, k_tile = q[:, cols], k_all[:, cols]
        v_t = v_all[:, cols].T
        mixed = []
        for odd in range(2):
            s = dot_nt(k_tile, lanes_of(q_tile, odd)) + bias[...]
            top = jnp.max(s, axis=0, keepdims=True)
            expo = jnp.exp(s - top)
            total = jnp.sum(expo, axis=0, keepdims=True)
            pb = (expo * (1.0 / total)).astype(BF)
            probs[2 * t + odd] = pb
            mixed.append(dot(v_t, pb))
        po[:, D + 128 * t : D + 128 * t + 128] = jnp.where(sub < HD, mixed[0], mixed[1]).T.astype(BF)
    h_t[...] = h_all[...].T
    half = pl.ds(pl.multiple_of(core * HALF, HALF), HALF)
    placed = dot(po[:, D:], pa[half, :]).astype(BF)
    po[:, :HALF] = dot(placed, weight_at(attn, 3)).astype(BF)
    po[:, HALF:D] = dot(placed, weight_at(attn, 4)).astype(BF)


def ffn_kernel(
    scal,
    chips,
    x,
    part_a,
    part_b,
    cot,
    cot_other,
    wanted,
    e2,
    g2,
    wg,
    wu,
    wd0,
    wd1,
    wd2,
    out_keep,
    dh2_out,
    resid,
    keep_g,
    send_g,
    keep_u,
    send_u,
    keep_d,
    send_d,
    h2p,
    h2p_t,
    dy,
    acc_out,
    acc_dh2,
    grad_d,
):
    core = scal[1]
    j = pl.program_id(0)

    @pl.when(j == 0)
    def _():
        r = x[...].astype(F32) + (part_a[...].astype(F32) + part_b[...].astype(F32))
        resid[...] = r
        scale = lax.rsqrt(jnp.mean(r * r, axis=1, keepdims=True) + EPS)
        h2 = (r * scale * g2[0:1, :]).astype(BF)
        h2p[:, :512] = dot(h2[:, :HALF], e2[...]).astype(BF)
        h2p[:, 512:] = dot(h2[:, HALF:], e2[...]).astype(BF)
        for k in range(2):
            h2p_t[k] = dot(h2, placed_matrix(wanted[k : k + 1, :])).astype(BF).T
        dy[pl.ds(pl.multiple_of(core * 128, 128), 128), :] = cot[...]
        dy[pl.ds(pl.multiple_of((1 - core) * 128, 128), 128), :] = cot_other[...]
        acc_out[...] = jnp.zeros_like(acc_out)
        acc_dh2[...] = jnp.zeros_like(acc_dh2)

    w_gate, w_up = wg[...].reshape(1024, HALF), wu[...].reshape(1024, HALF)
    gate, up = dot(h2p[...], w_gate), dot(h2p[...], w_up)
    blocks = jnp.concatenate([wd0[...], wd1[...], wd2[...]], axis=1).astype(F32)
    w_down = jnp.concatenate(
        [blocks[:, :, 0:8, :].reshape(HALF, HALF), blocks[:, :, 8:16, :].reshape(HALF, HALF)], axis=1
    ).astype(BF)
    sig = jax.nn.sigmoid(gate)
    hidden = (gate * sig * up).astype(BF)
    acc_out[...] += dot(hidden, w_down)
    dhid = dot_nt(dy[...], w_down)
    dgate = (dhid * up * sig * (1.0 + gate * (1.0 - sig))).astype(BF)
    dup = (dhid * gate * sig).astype(BF)
    acc_dh2[...] += dot_nt(dgate, w_gate) + dot_nt(dup, w_up)

    for part, value, keep, send in ((0, dgate, keep_g, send_g), (1, dup, keep_u, send_u)):
        grad = dot(h2p_t[part], value).astype(BF).reshape(8, 96, HALF)
        keep[...] = grad[:4]
        send[...] = grad[4:]
    grad_d[pl.ds(pl.multiple_of(j * HALF, HALF), HALF), :] = dot_tn(hidden, dy[...])

    @pl.when(j == 3)
    def _():
        mine = pl.multiple_of(core * 128, 128)
        other = pl.multiple_of((1 - core) * 128, 128)
        out_keep[...] = acc_out[pl.ds(mine, 128), :]
        dh2 = acc_dh2[...].astype(BF)
        dh2_out[:TOK, :HALF] = dot_nt(dh2[:, :512], e2[...]).astype(BF)
        dh2_out[:TOK, HALF:] = dot_nt(dh2[:, 512:], e2[...]).astype(BF)
        dh2_out[TOK:, :] = acc_out[pl.ds(other, 128), :].astype(BF)

        def write(w, carry):
            for at, out in ((w, keep_d), (w + 32, send_d)):
                base = chips[2, at] * 24
                for k in range(3):
                    rows = grad_d[pl.ds(pl.multiple_of(base + 8 * k, 8), 8), :]
                    out[w, k] = jnp.concatenate([rows[:, :HALF], rows[:, HALF:]], axis=0).astype(BF)
            return carry

        lax.fori_loop(0, 32, write, 0, unroll=2)


def attn_backward_kernel(
    scal,
    resid,
    dh2_a,
    dh2_b,
    g2,
    cot,
    cot_other,
    wo_a,
    wo_b,
    wanted,
    probs,
    o_mine,
    o_other,
    q,
    k_all,
    v_all,
    h_t,
    cosine,
    sine,
    dres_out,
    dq_out,
    dk_out,
    dv_out,
    grads,
    do,
    inner,
    grad_o,
    pa,
):
    core = scal[1]
    own = pl.ds(pl.multiple_of(scal[0] * TOK, TOK), TOK)
    step = pl.program_id(0)

    @pl.when(step == 0)
    def _():
        pa[...] = placed_matrix(wanted[3:4, :])
        r = resid[...]
        dh2 = dh2_a[...].astype(F32) + dh2_b[...].astype(F32)
        scale = lax.rsqrt(jnp.mean(r * r, axis=1, keepdims=True) + EPS)
        weighted = dh2 * g2[0:1, :]
        mean = jnp.mean(weighted * r, axis=1, keepdims=True)
        mine, theirs = cot[...].astype(F32), cot_other[...].astype(F32)
        dy = jnp.concatenate([jnp.where(core == 0, mine, theirs), jnp.where(core == 0, theirs, mine)], axis=0)
        dres = dy + (scale * weighted - r * (scale * scale * scale) * mean)
        dresb = dres.astype(BF)
        placed = dot_nt(dresb[:, :HALF], wo_a[...].reshape(D, HALF)) + dot_nt(dresb[:, HALF:], wo_b[...].reshape(D, HALF))
        half = pl.ds(pl.multiple_of(core * HALF, HALF), HALF)
        found = dot_nt(placed.astype(BF), pa[half, :]).astype(BF)
        head_of = (
            lax.broadcasted_iota(jnp.int32, (8, HALF), 1) // HD == lax.broadcasted_iota(jnp.int32, (8, HALF), 0)
        ).astype(F32)
        o_a, o_b = o_mine[...], o_other[...]
        inner[...] = lax.dot_general(
            head_of,
            found.astype(F32) * o_a.astype(F32),
            (((1,), (1,)), ((), ())),
            precision=lax.Precision.HIGHEST,
            preferred_element_type=F32,
        )
        o_full = jnp.concatenate([jnp.where(core == 0, o_a, o_b), jnp.where(core == 0, o_b, o_a)], axis=1)
        d_mine = jnp.where(core == 0, dresb[:, :HALF], dresb[:, HALF:])
        found_o = dot_tn(dot(o_full, pa[...]).astype(BF), d_mine).astype(BF)
        for t in range(3):
            do[t] = found[:, 128 * t : 128 * t + 128]
            grad_o[t] = found_o[:, 128 * t : 128 * t + 128].reshape(8, 96, 128)
        dres_out[0] = dres[0:128, :]
        dres_out[1] = dres[128:256, :]

    @pl.when(step > 0)
    def _():
        t = step - 1
        sub = lax.broadcasted_iota(jnp.int32, (128, TOK), 0)
        q_tile, do_tile, v_tile = q[...], do[t], v_all[...]
        k_t = k_all[...].T
        dqs, dks, dvs = [], [], []
        for odd in range(2):
            pb = probs[odd]
            dp = dot_nt(v_tile, lanes_of(do_tile, odd))
            ds = (pb.astype(F32) * (dp - inner[pl.ds(2 * t + odd, 1), :])).astype(BF)
            dks.append(dot(ds, q_tile))
            dvs.append(dot(pb, do_tile))
            dqs.append(dot(k_t, ds))
        u = jnp.where(sub < HD, dqs[0], dqs[1]).T * 0.125
        dq = (u * cosine[own, :] - swap_halves(u) * sine[own, :]).astype(BF)
        u = join_lanes(dks[0], dks[1])
        dk = (u * cosine[...] - swap_halves(u) * sine[...]).astype(BF)
        dv = join_lanes(dvs[0], dvs[1]).astype(BF)
        dq_out[...] = dq
        dk_out[...] = dk
        dv_out[...] = dv
        both = dot(h_t[...], jnp.concatenate([dk, dv], axis=1)).astype(BF)
        grads[:, 0:96, :] = dot(h_t[:, own], dq).astype(BF).reshape(8, 96, 128)
        grads[:, 96:192, :] = both[:, :128].reshape(8, 96, 128)
        grads[:, 192:288, :] = both[:, 128:].reshape(8, 96, 128)
        grads[:, 288:384, :] = grad_o[t]


def dh1_kernel(scal, dq, dk, dv, attn, wanted, out, pa):
    @pl.when(pl.program_id(0) == 0)
    def _():
        pa[...] = placed_matrix(wanted[3:4, :])

    wq, wk, wv = (weight_at(attn, k) for k in range(3))
    mine = jnp.where(scal[0] == pl.program_id(0), dq[...], jnp.zeros_like(dq))
    total = dot_nt(dk[...], wk) + dot_nt(dv[...], wv) + dot_nt(mine, wq)
    out[...] = dot_nt(total.astype(BF), pa[...]).astype(BF)


def terms_kernel(*refs):
    for k in range(3):
        total = (refs[2 * k][...].astype(F32) + refs[2 * k + 1][...].astype(F32)).astype(BF)
        half = total.shape[0] // 2
        refs[6 + 2 * k][...] = total[:half]
        refs[7 + 2 * k][...] = total[half:]


def padded_kernel(x0, y0, x1, y1, x2, y2, attn, out):
    pick = dense_rows()

    def write(at, rows):
        out[:, at] = dot_tn(pick, rows).astype(BF).reshape(8, 16, HALF)

    for at, x, y in ((0, x0, y0), (4, x1, y1)):
        total = (x[0].astype(F32) + y[0].astype(F32)).astype(BF)
        for k in range(4):
            write(at + k, total[96 * k : 96 * k + 96])
    out[:, 12:15] = (x2[0].astype(F32) + y2[0].astype(F32)).astype(BF).reshape(8, 3, 16, HALF)
    for k in range(4):
        rows = slice(96 * k, 96 * k + 96)
        total = attn[0, rows, :].astype(F32)
        for b in range(1, 8):
            total += attn[b, rows, :].astype(F32)
        write(8 + k, total.astype(BF))


def sum_kernel(scal, blocks, total, other):
    core = scal[1]
    for k in range(15):
        value = blocks[0, k].astype(F32)
        for b in range(1, 8):
            value += blocks[b, k].astype(F32)
        total[k] = value
        other[k] = jnp.where(core == 0, value[8:16], value[0:8])


def update_kernel(scal, mine, theirs, x_ref, dh1_ref, g1, dres, resid, out_a, out_b, *refs):
    core = scal[1]
    output, input_grad = refs[56:58]
    x = x_ref[...].astype(F32)
    dh1 = dh1_ref[...].astype(F32)
    scale = lax.rsqrt(jnp.mean(x * x, axis=1, keepdims=True) + EPS)
    weighted = dh1 * g1[0:1, :]
    inner = jnp.mean(weighted * x, axis=1, keepdims=True)
    input_grad[...] = dres[core] + (scale * weighted - x * (scale * scale * scale) * inner)
    tokens = pl.ds(pl.multiple_of(core * 128, 128), 128)
    output[...] = (resid[tokens, :] + (out_a[...] + out_b[TOK:, :].astype(F32))).astype(BF)
    masters, moments, averages = refs[0:8], refs[8:16], refs[16:24]
    news, moms, means, copies = refs[24:32], refs[32:40], refs[40:48], refs[48:56]
    base = 1.0 / math.sqrt(16384)

    def step(k, at, grad):
        rate = RATES[k] * base
        moment = MOMENTUM * moments[k][at] + grad
        new = masters[k][at] - rate * (grad + MOMENTUM * moment)
        news[k][at] = new
        moms[k][at] = moment
        means[k][at] = AVERAGE * averages[k][at] + (1.0 - AVERAGE) * new
        copies[k][at] = new.astype(BF)

    def halves(a, b):
        return (jnp.where(core == 0, a, b), jnp.where(core == 0, b, a))

    gain_sums = [jnp.zeros((6, 128), F32), jnp.zeros((6, 128), F32)]

    def weigh(which, k, at, grad):
        product = masters[k][at].astype(BF).astype(F32) * grad
        for c in range(0, product.shape[1], 128):
            gain_sums[which] += product[:, c : c + 128]

    own = pl.ds(pl.multiple_of(core * 8, 8), 8)

    def chunk(k):
        a, b = mine[k, own, :][0:6, :], theirs[k][0:6, :]
        return (jnp.where(core == 0, a, b), jnp.where(core == 0, b, a))

    for k, weight, offset, gain in (
        (8, 0, 0, 0),
        (9, 1, 0, 0),
        (10, 2, 0, 0),
        (11, 3, 0, None),
        (0, 4, 0, 1),
        (1, 4, D, 1),
        (2, 4, 2 * D, 1),
        (3, 4, 3 * D, 1),
        (4, 5, 0, 1),
        (5, 5, D, 1),
        (6, 5, 2 * D, 1),
        (7, 5, 3 * D, 1),
    ):
        for h, grad in enumerate(chunk(k)):
            at = (slice(0, 6), slice(offset + h * HALF, offset + (h + 1) * HALF))
            step(weight, at, grad)
            if gain is not None:
                weigh(gain, weight, at, grad)
    for j in range(3):
        for h in range(2):
            grad = mine[12 + j, 8 * h : 8 * h + 8, :]
            step(6, (slice(8 * j, 8 * j + 8), slice(h * HALF, (h + 1) * HALF)), grad)
    row = lax.broadcasted_iota(jnp.int32, (6, 128), 0)
    lane = lax.broadcasted_iota(jnp.int32, (6, 128), 1)
    for k in range(2):
        column = jnp.sum(gain_sums[k], axis=1, keepdims=True)
        line = jnp.sum(jnp.where(lane == row, column, 0.0), axis=0, keepdims=True)[:, 0:6]
        at = (slice(k, k + 1), slice(0, 6))
        step(7, at, line / masters[7][at].astype(BF).astype(F32))


def whole():
    return pl.BlockSpec(memory_space=pltpu.VMEM)


def scalars():
    return pl.BlockSpec(memory_space=pltpu.SMEM)


def call(kernel, out_shape, operands, scratch=(), smem=1, name=None, micros=1.0, mib=60):
    specs = [scalars() if k < smem else whole() for k in range(len(operands))]
    return pl.pallas_call(
        kernel,
        out_shape=out_shape,
        in_specs=specs,
        out_specs=jax.tree.map(lambda _: whole(), out_shape),
        scratch_shapes=list(scratch),
        compiler_params=params(mib),
        cost_estimate=cost(micros),
        name=name,
    )(*operands)


def shape(dims, kind):
    return jax.ShapeDtypeStruct(dims, kind)


def add(a, b):
    return (a.astype(F32) + b.astype(F32)).astype(BF)


def fetch(block, axis):
    return permute(block, flip_pairs(axis, 3))


def first_terms(parts):
    return [fetch(send, order[0]) for order, (_, send) in reversed(list(zip(ORDERS, parts)))][::-1]


def next_terms(keeps, got):
    count, rows = keeps[0].shape[0], 96
    pair = [pl.BlockSpec((count // 2, rows, HALF), lambda j: (0, j, 0))] * 6
    out = pl.pallas_call(
        terms_kernel,
        out_shape=(shape((count // 2, HALF, HALF), BF),) * 6,
        grid=(HALF // rows,),
        in_specs=[pl.BlockSpec((count, rows, HALF), lambda j: (0, j, 0))] * 6,
        out_specs=tuple(pair),
        compiler_params=params(),
        cost_estimate=cost(1),
        name="next_terms",
    )(*(v for pair in zip(keeps, got) for v in pair))
    return out[::2], out[1::2]


def reduce_rows(parts, got, after):
    keeps, sents = next_terms([keep for keep, _ in parts], got)
    got = [fetch(sent, order[1]) for sent, order in zip(sents, ORDERS)]
    got, after = lax.optimization_barrier((got, after))
    keeps, sents = next_terms(keeps, got)
    got = [fetch(sent, order[2]) for sent, order in zip(sents, ORDERS)]
    return [term for pair in zip(keeps, got) for term in pair], after


def flipped(block, flip):
    return permute(block, flip_pairs("z", flip))


def shards(inputs, doc_ids, cotangent, *state):
    state = tuple(v.T if k % 8 == 7 else v for k, v in enumerate(state))
    masters, moments, averages = state[0:8], state[8:16], state[16:24]
    z, core = lax.axis_index("z"), lax.axis_index("core")
    y, x_at = lax.axis_index("y"), lax.axis_index("x")
    scal = jnp.stack([z, core]).astype(jnp.int32)
    chips = chip_of_place({"z": z, "y": y, "x": x_at}, core)

    halves = shape((8, 8, HALF), F32)
    wq, wk, wv, wo, wg, wu, wd, gains = masters
    keep, send = call(pack_ffn_kernel, (halves, halves), (scal, wg, wu), name="pack_feed_forward")
    ffn_w = call(
        merge_ffn_kernel,
        shape((11, 16, HALF), BF),
        (scal, keep, permute(send, CORE_PAIRS), wd),
        name="merge_feed_forward",
    )
    ffn_w, wq, wk, wv, wo, gains, inputs, doc_ids, cotangent = lax.optimization_barrier(
        (ffn_w, wq, wk, wv, wo, gains, inputs, doc_ids, cotangent)
    )
    ffn_w = lax.all_gather(ffn_w, ("z", "y", "x"), axis=0, tiled=False)
    halves = shape((5, 8, HALF), F32)
    keep, send = call(
        pack_attn_kernel,
        (halves, halves),
        (scal, wq, wk, wv, wo, gains),
        scratch=(pltpu.VMEM((8, 128), F32),),
        name="pack_attention",
    )
    theirs, cot_other = permute(send, CORE_PAIRS), permute(cotangent[0], CORE_PAIRS)
    theirs, cot_other = lax.optimization_barrier((theirs, cot_other))
    attn = call(merge_attn_kernel, shape((8, 5, 16, HALF), BF), (scal, keep, theirs), name="merge_attention")

    ids_row = jnp.zeros((16, D), BF).at[0, :128].set(doc_ids[0].astype(BF))
    block = jnp.concatenate([inputs[0], ids_row], axis=0)
    attn, block = lax.optimization_barrier((attn, block))
    attn = exchange(attn, 1)
    seq = [block, flipped(block, 1), flipped(block, 3)]
    e2 = spread_matrix()
    wanted = placed_features(chips)
    attn, wanted, chips, e2 = lax.optimization_barrier((attn, wanted, chips, e2))
    attn = call(dense_kernel, shape((8, 512, HALF), BF), (attn,), smem=0, name="dense_rows", mib=16)
    attn = exchange(attn, 3)
    seq.append(flipped(seq[1], 3))
    seq = jnp.stack(seq)
    seq_other = permute(seq, CORE_PAIRS)
    ids = jnp.concatenate([seq[:, 128, :128], seq_other[:, 128, :128]], axis=0).astype(F32)
    spots = [(((z + c) % 4 ^ flip) + 4 - c) % 4 * 2 + c for c in (core, 1 - core) for flip in FLIPS]
    here = jnp.stack(spots)[None, :] == jnp.arange(8)[:, None]
    ids = jnp.sum(jnp.where(here[:, :, None], ids[None], 0.0), axis=1).reshape(LEN)
    starts = jnp.sum((ids[None, :] < ids[:, None]).astype(jnp.int32), axis=1)
    freq = 10000.0 ** (-jnp.arange(0, HD, 2, dtype=F32) / HD)
    spot = (jnp.arange(LEN, dtype=jnp.int32) - starts).astype(F32)
    theta = spot[:, None] * jnp.tile(freq, 4)[None, :]
    sign = jnp.tile(jnp.repeat(jnp.array([-1.0, 1.0], F32), HD // 2), 2)
    cosine, sine = jnp.cos(theta), jnp.sin(theta) * sign[None, :]
    start_row = jnp.broadcast_to(starts.astype(F32)[None, :], (8, LEN))

    q, k_all, v_all, h_all, h_t, x_chip, probs, po, g1, g2 = call(
        attn_forward_kernel,
        (
            shape((TOK, HALF), BF),
            shape((LEN, HALF), BF),
            shape((LEN, HALF), BF),
            shape((LEN, D), BF),
            shape((D, LEN), BF),
            shape((TOK, D), BF),
            shape((HEADS, LEN, TOK), BF),
            shape((TOK, D + HALF), BF),
            shape((8, D), F32),
            shape((8, D), F32),
        ),
        (scal, seq, seq_other, cosine, sine, start_row, wanted, attn),
        scratch=(pltpu.VMEM((LEN, D), BF), pltpu.VMEM((LEN, TOK), F32), pltpu.VMEM((D, D), BF)),
        name="attention_forward",
        micros=1.3e7,
    )
    po_other = permute(po, CORE_PAIRS)

    def full(dims):
        return pl.BlockSpec(dims, lambda i, n=len(dims): (0,) * n)

    ffn_out = (
        shape((128, D), F32),
        shape((TOK + 128, D), BF),
        shape((TOK, D), F32),
    ) + tuple(shape((4, HALF, HALF), BF) for _ in range(4)) + tuple(shape((32, 3, 16, HALF), BF) for _ in range(2))
    column = pl.BlockSpec((4, 96, HALF), lambda j: (0, j, 0))
    out_keep, dh2, resid, kg, sg, ku, su, kd, sd = pl.pallas_call(
        ffn_kernel,
        out_shape=ffn_out,
        grid=(4,),
        in_specs=[
            scalars(),
            scalars(),
            full((TOK, D)),
            full((TOK, D)),
            full((TOK, D)),
            full((128, D)),
            full((128, D)),
            full((8, D)),
            full((HALF, 512)),
            full((8, D)),
            pl.BlockSpec((64, 1, 16, HALF), lambda j: (0, j, 0, 0)),
            pl.BlockSpec((64, 1, 16, HALF), lambda j: (0, 4 + j, 0, 0)),
            *(pl.BlockSpec((16, 1, 16, HALF), lambda j, k=k: (j, 8 + k, 0, 0)) for k in range(3)),
        ],
        out_specs=tuple(full(s.shape) for s in ffn_out[:3])
        + (column,) * 4
        + tuple(full(s.shape) for s in ffn_out[7:]),
        scratch_shapes=[
            pltpu.VMEM((TOK, 1024), BF),
            pltpu.VMEM((2, D, TOK), BF),
            pltpu.VMEM((TOK, D), BF),
            pltpu.VMEM((TOK, D), F32),
            pltpu.VMEM((TOK, 1024), F32),
            pltpu.VMEM((FF // 2, D), F32),
        ],
        compiler_params=params(),
        cost_estimate=cost(4),
        name="feed_forward",
    )(
        scal,
        chips,
        x_chip,
        po,
        po_other,
        cotangent[0],
        cot_other,
        wanted,
        e2,
        g2,
        *((ffn_w,) * 5),
    )

    dh2_other = permute(dh2, CORE_PAIRS)
    dh2_other, kg, sg, ku, su, kd, sd = lax.optimization_barrier((dh2_other, kg, sg, ku, su, kd, sd))
    at_tile = lambda i: jnp.maximum(i - 1, 0)
    short = pl.BlockSpec((TOK, 128), lambda i: (0, at_tile(i)))
    long = pl.BlockSpec((LEN, 128), lambda i: (0, at_tile(i)))
    dres, dq, dk, dv, grads = pl.pallas_call(
        attn_backward_kernel,
        out_shape=(
            shape((2, 128, D), F32),
            shape((TOK, HALF), BF),
            shape((LEN, HALF), BF),
            shape((LEN, HALF), BF),
            shape((8, HALF, HALF), BF),
        ),
        grid=(4,),
        in_specs=[
            scalars(),
            full((TOK, D)),
            full((TOK, D)),
            full((TOK, D)),
            full((8, D)),
            full((128, D)),
            full((128, D)),
            pl.BlockSpec((8, 96, HALF), lambda i: (0, 3, 0)),
            pl.BlockSpec((8, 96, HALF), lambda i: (0, 4, 0)),
            full((8, D)),
            pl.BlockSpec((2, LEN, TOK), lambda i: (at_tile(i), 0, 0)),
            pl.BlockSpec((TOK, HALF), lambda i: (0, 2)),
            pl.BlockSpec((TOK, HALF), lambda i: (0, 2)),
            short,
            long,
            long,
            full((D, LEN)),
            full((LEN, 128)),
            full((LEN, 128)),
        ],
        out_specs=(
            full((2, 128, D)),
            short,
            long,
            long,
            pl.BlockSpec((8, HALF, 128), lambda i: (0, 0, at_tile(i))),
        ),
        scratch_shapes=[
            pltpu.VMEM((3, TOK, 128), BF),
            pltpu.VMEM((8, TOK), F32),
            pltpu.VMEM((3, 8, 96, 128), BF),
            pltpu.VMEM((D, D), BF),
        ],
        compiler_params=params(),
        cost_estimate=cost(1),
        name="attention_backward",
    )(
        scal,
        resid,
        dh2,
        dh2_other,
        g2,
        cotangent[0],
        cot_other,
        attn,
        attn,
        wanted,
        probs,
        po,
        po_other,
        q,
        k_all,
        v_all,
        h_t,
        cosine,
        sine,
    )
    parts = [(kg, sg), (ku, su), (kd.reshape(4, HALF, HALF), sd.reshape(4, HALF, HALF))]
    got = first_terms(parts)
    grads, dq, dk, dv, got = lax.optimization_barrier((grads, dq, dk, dv, got))
    grads = exchange(grads, 3)
    dh1 = pl.pallas_call(
        dh1_kernel,
        out_shape=shape((LEN, D), BF),
        grid=(4,),
        in_specs=[
            scalars(),
            full((TOK, HALF)),
            pl.BlockSpec((TOK, HALF), lambda b: (b, 0)),
            pl.BlockSpec((TOK, HALF), lambda b: (b, 0)),
            pl.BlockSpec((8, 288, HALF), lambda b: (0, 0, 0)),
            full((8, D)),
        ],
        out_specs=pl.BlockSpec((TOK, D), lambda b: (b, 0)),
        scratch_shapes=[pltpu.VMEM((D, D), BF)],
        compiler_params=params(),
        cost_estimate=cost(1),
        name="attention_input_gradient",
    )(scal, dq, dk, dv, attn, wanted)
    terms, dh1 = reduce_rows(parts, got, dh1)
    dh1 = lax.psum_scatter(dh1, ("z", "core"), scatter_dimension=0, tiled=True)
    blocks = call(padded_kernel, shape((8, 15, 16, HALF), BF), (*terms, grads), smem=0, name="padded_rows")
    blocks = exchange(blocks, 1)

    grads, theirs = call(
        sum_kernel, (shape((15, 16, HALF), F32), shape((15, 8, HALF), F32)), (scal, blocks), name="sum_blocks", mib=16
    )
    theirs = permute(theirs, CORE_PAIRS)
    shapes = tuple(shape(m.shape, F32) for m in masters)
    outs = call(
        update_kernel,
        shapes * 3 + tuple(shape(m.shape, BF) for m in masters) + (shape((128, D), BF), shape((128, D), F32)),
        (scal, grads, theirs, inputs[0], dh1, g1, dres, resid, out_keep, dh2_other, *masters, *moments, *averages),
        name="update",
    )
    outs, output, input_grad = outs[:32], *outs[32:]
    outs = tuple(v.T if k % 8 == 7 else v for k, v in enumerate(outs))
    return (output[None], input_grad[None], *outs)


def solution(mesh):
    fine = Mesh(mesh.devices.reshape(4, 2, 4, 4), AXES)
    tokens = P(("y", "x"), ("z", "core"), None)
    rows = P(("z", "core", "y", "x"), None)
    return jax.shard_map(
        shards,
        mesh=fine,
        in_specs=(tokens, P(("y", "x"), ("z", "core")), tokens) + (rows,) * 24,
        out_specs=(tokens, tokens) + (rows,) * 32,
        check_vma=False,
    )
```

profile of v0, /device:TPU:1, one launch (start us, length us, event | category | flops | bytes accessed | tf_op | source)
XLA Modules:
  0.0 233.6 jit_solution(5429324111819382689)
XLA Ops:
  7.9 1.6 pack_feed_forward.1
  9.6 1.4 collective-permute-start
  12.8 1.7 merge_feed_forward.1
  17.1 1.5 pack_attention.1
  18.9 1.3 collective-permute-done.1.other
  20.8 1.7 merge_attention.1
  22.5 11.9 %all-to-all-start = ((bf16[8,5,16,384]{3,2,1,0:T(8,128)(2,1)}), bf16[8,5,16,384]{3,2,1,0:T(8,128)(2,1)S(1)}, u32[]{:S(2)}, u32[]{:S(2)}) async-start(bf16[8,5,16,384]{3,2,1,0:T(8,128)(2,1)} %merge_attention.1), calls=%async_computation | async-start | bytes 983040 | tf_op jit(solution)/shard_map/all_to_all | solution.py:85
  35.9 2.9 %all-to-all-done.blocks = bf16[8,5,16,384]{3,2,1,0:T(8,128)(2,1)S(1)} async-done(((bf16[8,5,16,384]{3,2,1,0:T(8,128)(2,1)}), bf16[8,5,16,384]{3,2,1,0:T(8,128)(2,1)S(1)}, u32[]{:S(2)}, u32[]{:S(2)}) %all-to-all-start) | async-done | bytes 491552 | tf_op jit(solution)/shard_map/all_to_all | solution.py:85
  38.8 2.1 dense_rows.1
  41.0 3.6 %all-to-all-start.1 = ((bf16[8,512,384]{2,1,0:T(8,128)(2,1)}), bf16[8,512,384]{2,1,0:T(8,128)(2,1)S(1)}, u32[]{:S(2)}, u32[]{:S(2)}) async-start(bf16[8,512,384]{2,1,0:T(8,128)(2,1)} %dense_rows.1), calls=%async_computation.1 | async-start | bytes 6291456 | tf_op jit(solution)/shard_map/all_to_all | solution.py:85
  44.6 2.4 %collective-permute-start.3 = (bf16[144,768]{1,0:T(8,128)(2,1)S(1)}, bf16[144,768]{1,0:T(8,128)(2,1)S(1)}, u32[]{:S(2)}, u32[]{:S(2)}) collective-permute-start(bf16[144,768]{1,0:T(8,128)(2,1)S(1)} %fusion.3), channel_id=1, source_target_pairs={{0,32},{1,33},{2,34},{3,35},{4,36},{5,37},{6,38},{7,39},{8,40},{9,... | collective-permute-start | bytes 663560 | tf_op jit(solution)/shard_map/ppermute | solution.py:68
  47.7 6.6 %collective-permute-done.3 = bf16[144,768]{1,0:T(8,128)(2,1)S(1)} collective-permute-done((bf16[144,768]{1,0:T(8,128)(2,1)S(1)}, bf16[144,768]{1,0:T(8,128)(2,1)S(1)}, u32[]{:S(2)}, u32[]{:S(2)}) %collective-permute-start.3) | collective-permute-done | bytes 221216 | tf_op jit(solution)/shard_map/ppermute | solution.py:68
  54.9 20.0 %collective-permute-done.4 = bf16[144,768]{1,0:T(8,128)(2,1)S(1)} collective-permute-done((bf16[144,768]{1,0:T(8,128)(2,1)S(1)}, bf16[144,768]{1,0:T(8,128)(2,1)S(1)}, u32[]{:S(2)}, u32[]{:S(2)}) %collective-permute-start.4) | collective-permute-done | bytes 221216 | tf_op jit(solution)/shard_map/ppermute | solution.py:68
  74.9 2.3 collective-permute-done.5
  78.3 1.6 collective-permute-start.6
  83.6 3.1 %fusion.1 = (f32[1024,128]{1,0:T(8,128)}, f32[1024,128]{1,0:T(8,128)}) fusion(f32[128]{0:T(128)S(1)} %mul.213, f32[128]{0:T(128)S(1)} %mul.210, f32[1024]{0:T(1024)S(1)} %get-tuple-element.269), kind=kLoop, calls=%fused_computation.6 | loop fusion | flops 262144 | bytes 1053696 | tf_op jit(solution)/shard_map/mul | solution.py:741
  88.3 16.4 %attention_forward.1 = (bf16[256,384]{1,0:T(8,128)(2,1)}, bf16[1024,384]{1,0:T(8,128)(2,1)}, bf16[1024,384]{1,0:T(8,128)(2,1)}, bf16[1024,768]{1,0:T(8,128)(2,1)...) custom-call(s32[2]{0:T(128)} %pad_add_fusion.1.scal, ...), custom_call_target="tpu_custom_call" | custom-call | flops 13000000512 | bytes 1 | tf_op jit(solution)/shard_map/attention_forward/pallas_call | solution.py:629
  105.1 1.8 collective-permute-done.7.part_b.o_other
  107.0 3.2 %all-gather.3.cloned.1.call-done = bf16[704,16,384]{2,1,0:T(8,128)(2,1)} async-done(((bf16[11,16,384]{2,1,0:T(8,128)(2,1)}), bf16[704,16,384]{2,1,0:T(8,128)(2,1)}) %all-gather.3.cloned.1.call-update) | async-done | bytes 8650768 | tf_op jit(solution)/shard_map/all_gather | solution.py:706
  110.2 17.2 %feed_forward.1 = (f32[128,768]{1,0:T(8,128)}, bf16[384,768]{1,0:T(8,128)(2,1)}, f32[256,768]{1,0:T(8,128)}, bf16[4,384,384]{2,1,0:T(8,128)(2,1)}, bf16[4,384,38...) custom-call(s32[2]{0:T(128)} %pad_add_fusion.1.scal, ...), custom_call_target="tpu_custom_call" | custom-call | flops 4001 | bytes 1 | tf_op jit(solution)/shard_map/feed_forward/pallas_call | solution.py:774
  128.1 1.8 collective-permute-done.8.dh2_b.out_b
  132.3 14.5 %attention_backward.1 = (f32[2,128,768]{2,1,0:T(8,128)}, bf16[256,384]{1,0:T(8,128)(2,1)}, bf16[1024,384]{1,0:T(8,128)(2,1)}, bf16[1024,384]{1,0:T(8,128)(2,1)}, bf16[8,384,384]{2,1,0:T(8,128)(2,1)}) custom-call(s32[2]{0:T(128)} %pad_add_fusion.1.scal, f32[256,768]{1,0:T(8,128)} %get-tuple-element.188.resid, bf16[384,768]{1,0:T(8,128)(2,1)} %get-tuple-element.180.dh2_a, ...), custom_call_target="tpu_custom_call" | custom-call | flops 1001 | bytes 1 | tf_op jit(solution)/shard_map/attention_backward/pallas_call | solution.py:826
  148.9 5.5 %next_terms.2 = (bf16[2,384,384]{2,1,0:T(8,128)(2,1)}, bf16[2,384,384]{2,1,0:T(8,128)(2,1)}, bf16[2,384,384]{2,1,0:T(8,128)(2,1)}, bf16[2,384,384]{2,1,0:T(8,128...) custom-call(bf16[4,384,384]{2,1,0:T(8,128)(2,1)} %get-tuple-element.187.refs_0_, ...), custom_call_target="tpu_custom_call" | custom-call | flops 1001 | bytes 1 | tf_op jit(solution)/shard_map/next_terms/pallas_call | solution.py:660
  156.2 3.6 %all-to-all-start.2 = ((bf16[8,384,384]{2,1,0:T(8,128)(2,1)}), bf16[8,384,384]{2,1,0:T(8,128)(2,1)S(1)}, u32[]{:S(2)}, u32[]{:S(2)}) async-start(bf16[8,384,384]{2,1,0:T(8,128)(2,1)} %get-tuple-element.225), calls=%async_computation.2 | async-start | bytes 4718592 | tf_op jit(solution)/shard_map/all_to_all | solution.py:85
  160.1 7.9 %attention_input_gradient.1 = bf16[1024,768]{1,0:T(8,128)(2,1)} custom-call(s32[2]{0:T(128)} %pad_add_fusion.1.scal, bf16[256,384]{1,0:T(8,128)(2,1)} %get-tuple-element.211.dq, bf16[1024,384]{1,0:T(8,128)(2,1)} %get-tuple-element.212.dk, bf16[1024,384]{1,0:T(8,128)(2,1)} %get-tuple-element.213.dv, bf16[8,512,384]{2,1,0:T(8,128)(2,1)} %copy-done.2, ...), custom_call_target="tpu_custom_call" | custom-call | flops 1001 | bytes 1 | tf_op jit(solution)/shard_map/attention_input_gradient/pallas_call | solution.py:898
  169.0 4.0 %next_terms.3 = (bf16[1,384,384]{2,1,0:T(8,128)(2,1)}, bf16[1,384,384]{2,1,0:T(8,128)(2,1)}, bf16[1,384,384]{2,1,0:T(8,128)(2,1)}, bf16[1,384,384]{2,1,0:T(8,128...) custom-call(bf16[2,384,384]{2,1,0:T(8,128)(2,1)} %get-tuple-element.207.refs_0_, ...), custom_call_target="tpu_custom_call" | custom-call | flops 1001 | bytes 1 | tf_op jit(solution)/shard_map/next_terms/pallas_call | solution.py:660
  175.4 1.3 collective-permute-start.17
  176.6 5.2 %collective-permute-done.15.y0 = bf16[1,384,384]{2,1,0:T(8,128)(2,1)S(1)} collective-permute-done((bf16[1,384,384]{2,1,0:T(8,128)(2,1)}, bf16[1,384,384]{2,1,0:T(8,128)(2,1)S(1)}, u32[]{:S(2)}, u32[]{:S(2)}) %collective-permute-start.15) | collective-permute-done | bytes 294944 | tf_op jit(solution)/shard_map/ppermute | solution.py:68
  184.3 4.2 %padded_rows.1 = bf16[8,15,16,384]{3,2,1,0:T(8,128)(2,1)} custom-call(bf16[1,384,384]{2,1,0:T(8,128)(2,1)} %get-tuple-element.219.x0, bf16[1,384,384]{2,1,0:T(8,128)(2,1)} %copy-done.13, bf16[1,384,384]{2,1,0:T(8,128)(2,1)} %get-tuple-element.221.x1, bf16[1,384,384]{2,1,0:T(8,128)(2,1)} %copy-done.14, bf16[1,384,384]{2,1,0:T(8,128)(2,1)} %get-tuple-element.223.x2, ...), custom_call_target="tpu_custom_call" | custom-call | flops 1001 | bytes 1 | tf_op jit(solution)/shard_map/padded_rows/pallas_call | solution.py:629
  188.5 19.8 %all_to_all.20.blocks = bf16[8,15,16,384]{3,2,1,0:T(8,128)(2,1)S(1)} all-to-all(bf16[8,15,16,384]{3,2,1,0:T(8,128)(2,1)} %padded_rows.1), channel_id=1, replica_groups={{0,1,4,5,32,33,36,37},{2,3,6,7,34,35,38,39},{8,9,12,13,40,41,44,45},{10..., dimensions={0} | all-to-all | bytes 2949120 | tf_op jit(solution)/shard_map/all_to_all | solution.py:85
  209.8 11.4 %collective-permute-start.18 = (f32[15,8,384]{2,1,0:T(8,128)S(1)}, f32[15,8,384]{2,1,0:T(8,128)S(1)}, u32[]{:S(2)}, u32[]{:S(2)}) collective-permute-start(f32[15,8,384]{2,1,0:T(8,128)S(1)} %get-tuple-element.227), channel_id=1, source_target_pairs={{0,16},{1,17},{2,18},{3,19},{4,20},{5,21},{6,22},{7,23},{8,24},{9,... | collective-permute-start | bytes 552968 | tf_op jit(solution)/shard_map/ppermute | solution.py:68
  222.9 3.8 %update.1 = (f32[6,768]{1,0:T(8,128)}, f32[6,768]{1,0:T(8,128)}, f32[6,768]{1,0:T(8,128)}, f32[6,768]{1,0:T(8,128)}, f32[6,3072]{1,0:T(8,128)}, /*index=5*/f32[6...) custom-call(s32[2]{0:T(128)} %pad_add_fusion.1.scal, ...), custom_call_target="tpu_custom_call" | custom-call | flops 1001 | bytes 1 | tf_op jit(solution)/shard_map/update/pallas_call | solution.py:629
  (114 shorter events, 31.7 us)
Async XLA Ops:
  7.2 11.4 %copy-start.19 = (s32[1,128]{1,0:T(1,128)S(1)}, s32[1,128]{1,0:T(1,128)}, u32[]{:S(2)}) copy-start(s32[1,128]{1,0:T(1,128)} %param.55) | copy-start | bytes 1540
  7.2 11.7 %copy-start.10 = (bf16[1,128,768]{2,1,0:T(8,128)(2,1)S(1)}, bf16[1,128,768]{2,1,0:T(8,128)(2,1)}, u32[]{:S(2)}) copy-start(bf16[1,128,768]{2,1,0:T(8,128)(2,1)} %param.54) | copy-start | bytes 589828
  7.2 102.9 %all-gather.3.cloned.1.call-start = ((), (), s32[]{:S(2)}) async-start(), calls=%async_computation.6 | async-start | bytes 8785920 | tf_op jit(solution)/shard_map/all_gather | solution.py:706
  9.6 2.6 %collective-permute-start = (f32[8,8,384]{2,1,0:T(8,128)}, f32[8,8,384]{2,1,0:T(8,128)S(1)}, u32[]{:S(2)}, u32[]{:S(2)}) collective-permute-start(f32[8,8,384]{2,1,0:T(8,128)} %get-tuple-element.157), channel_id=1, source_target_pairs={{0,16},{1,17},{2,18},{3,19},{4,20},{5,21},{6,22},{7,23},{8,24},{9,... | collective-permute-start | bytes 294920 | tf_op jit(solution)/shard_map/ppermute | solution.py:68
  15.6 4.6 %collective-permute-start.2 = (bf16[128,768]{1,0:T(8,128)(2,1)}, bf16[128,768]{1,0:T(8,128)(2,1)S(1)}, u32[]{:S(2)}, u32[]{:S(2)}) collective-permute-start(bf16[128,768]{1,0:T(8,128)(2,1)} %bitcast.50), channel_id=1, source_target_pairs={{0,16},{1,17},{2,18},{3,19},{4,20},{5,21},{6,22},{7,23},{8,24},{9,... | collective-permute-start | bytes 589832 | tf_op jit(solution)/shard_map/ppermute | solution.py:68
  18.6 1.5 collective-permute-start.1
  20.2 2.3 copy-start.9
  22.5 16.3 %all-to-all-start = ((bf16[8,5,16,384]{3,2,1,0:T(8,128)(2,1)}), bf16[8,5,16,384]{3,2,1,0:T(8,128)(2,1)S(1)}, u32[]{:S(2)}, u32[]{:S(2)}) async-start(bf16[8,5,16,384]{3,2,1,0:T(8,128)(2,1)} %merge_attention.1), calls=%async_computation | async-start | bytes 983040 | tf_op jit(solution)/shard_map/all_to_all | solution.py:85
  41.0 45.7 %all-to-all-start.1 = ((bf16[8,512,384]{2,1,0:T(8,128)(2,1)}), bf16[8,512,384]{2,1,0:T(8,128)(2,1)S(1)}, u32[]{:S(2)}, u32[]{:S(2)}) async-start(bf16[8,512,384]{2,1,0:T(8,128)(2,1)} %dense_rows.1), calls=%async_computation.1 | async-start | bytes 6291456 | tf_op jit(solution)/shard_map/all_to_all | solution.py:85
  44.6 35.2 %copy-start.20 = (f32[2]{0:T(128)S(1)}, f32[2]{0:T(128)}, u32[]{:S(2)}) copy-start(f32[2]{0:T(128)} %constant.333.clone) | copy-start | bytes 28
  44.6 9.7 %collective-permute-start.3 = (bf16[144,768]{1,0:T(8,128)(2,1)S(1)}, bf16[144,768]{1,0:T(8,128)(2,1)S(1)}, u32[]{:S(2)}, u32[]{:S(2)}) collective-permute-start(bf16[144,768]{1,0:T(8,128)(2,1)S(1)} %fusion.3), channel_id=1, source_target_pairs={{0,32},{1,33},{2,34},{3,35},{4,36},{5,37},{6,38},{7,39},{8,40},{9,... | collective-permute-start | bytes 663560 | tf_op jit(solution)/shard_map/ppermute | solution.py:68
  47.0 28.0 %collective-permute-start.4 = (bf16[144,768]{1,0:T(8,128)(2,1)S(1)}, bf16[144,768]{1,0:T(8,128)(2,1)S(1)}, u32[]{:S(2)}, u32[]{:S(2)}) collective-permute-start(bf16[144,768]{1,0:T(8,128)(2,1)S(1)} %fusion.3), channel_id=1, source_target_pairs={{0,96},{1,97},{2,98},{3,99},{4,100},{5,101},{6,102},{7,103},{8,104... | collective-permute-start | bytes 663560 | tf_op jit(solution)/shard_map/ppermute | solution.py:68
  54.3 22.9 %collective-permute-start.5 = (bf16[144,768]{1,0:T(8,128)(2,1)S(1)}, bf16[144,768]{1,0:T(8,128)(2,1)S(1)}, u32[]{:S(2)}, u32[]{:S(2)}) collective-permute-start(bf16[144,768]{1,0:T(8,128)(2,1)S(1)} %collective-permute-done.3), channel_id=1, source_target_pairs={{0,96},{1,97},{2,98},{3,99},{4,100},{5,101},{6,102},{7,103},{8,104... | collective-permute-start | bytes 663560 | tf_op jit(solution)/shard_map/ppermute | solution.py:68
  78.3 4.0 %collective-permute-start.6 = (bf16[4,144,768]{2,1,0:T(8,128)(2,1)}, bf16[4,144,768]{2,1,0:T(8,128)(2,1)}, u32[]{:S(2)}, u32[]{:S(2)}) collective-permute-start(bf16[4,144,768]{2,1,0:T(8,128)(2,1)} %pad_maximum_fusion.seq), channel_id=1, source_target_pairs={{0,16},{1,17},{2,18},{3,19},{4,20},{5,21},{6,22},{7,23},{8,24},{9,... | collective-permute-start | bytes 2654216 | tf_op jit(solution)/shard_map/ppermute | solution.py:68
  86.7 1.7 copy-start.2
  104.7 2.2 collective-permute-start.7
  107.0 3.2 %copy-start.5 = (bf16[256,1152]{1,0:T(8,128)(2,1)}, bf16[256,1152]{1,0:T(8,128)(2,1)S(1)}, u32[]{:S(2)}) copy-start(bf16[256,1152]{1,0:T(8,128)(2,1)S(1)} %collective-permute-done.7.part_b.o_other) | copy-start | bytes 1769476
  127.3 2.6 %collective-permute-start.8 = (bf16[384,768]{1,0:T(8,128)(2,1)}, bf16[384,768]{1,0:T(8,128)(2,1)S(1)}, u32[]{:S(2)}, u32[]{:S(2)}) collective-permute-start(bf16[384,768]{1,0:T(8,128)(2,1)} %get-tuple-element.180.dh2_a), channel_id=1, source_target_pairs={{0,16},{1,17},{2,18},{3,19},{4,20},{5,21},{6,22},{7,23},{8,24},{9,... | collective-permute-start | bytes 1769480 | tf_op jit(solution)/shard_map/ppermute | solution.py:68
  129.9 2.4 %copy-start.4 = (bf16[384,768]{1,0:T(8,128)(2,1)}, bf16[384,768]{1,0:T(8,128)(2,1)S(1)}, u32[]{:S(2)}) copy-start(bf16[384,768]{1,0:T(8,128)(2,1)S(1)} %collective-permute-done.8.dh2_b.out_b) | copy-start | bytes 1769476
  129.9 16.9 %collective-permute-start.9 = (bf16[4,384,384]{2,1,0:T(8,128)(2,1)}, bf16[4,384,384]{2,1,0:T(8,128)(2,1)S(1)}, u32[]{:S(2)}, u32[]{:S(2)}) collective-permute-start(bf16[4,384,384]{2,1,0:T(8,128)(2,1)} %get-tuple-element.199), channel_id=1, source_target_pairs={{0,3},{1,2},{2,1},{3,0},{4,7},{5,6},{6,5},{7,4},{8,11},{9,10},{10,... | collective-permute-start | bytes 3538952 | tf_op jit(solution)/shard_map/ppermute | solution.py:68
  131.1 15.7 %collective-permute-start.10 = (bf16[4,384,384]{2,1,0:T(8,128)(2,1)}, bf16[4,384,384]{2,1,0:T(8,128)(2,1)S(1)}, u32[]{:S(2)}, u32[]{:S(2)}) collective-permute-start(bf16[4,384,384]{2,1,0:T(8,128)(2,1)} %get-tuple-element.200), channel_id=1, source_target_pairs={{0,12},{1,13},{2,14},{3,15},{4,8},{5,9},{6,10},{7,11},{8,4},{9,5},... | collective-permute-start | bytes 3538952 | tf_op jit(solution)/shard_map/ppermute | solution.py:68
  132.3 15.6 %collective-permute-start.11 = (bf16[4,384,384]{2,1,0:T(8,128)(2,1)}, bf16[4,384,384]{2,1,0:T(8,128)(2,1)S(1)}, u32[]{:S(2)}, u32[]{:S(2)}) collective-permute-start(bf16[4,384,384]{2,1,0:T(8,128)(2,1)} %bitcast.65), channel_id=1, source_target_pairs={{0,96},{1,97},{2,98},{3,99},{4,100},{5,101},{6,102},{7,103},{8,104... | collective-permute-start | bytes 3538952 | tf_op jit(solution)/shard_map/ppermute | solution.py:68
  154.4 13.6 %collective-permute-start.12 = (bf16[2,384,384]{2,1,0:T(8,128)(2,1)}, bf16[2,384,384]{2,1,0:T(8,128)(2,1)S(1)}, u32[]{:S(2)}, u32[]{:S(2)}) collective-permute-start(bf16[2,384,384]{2,1,0:T(8,128)(2,1)} %get-tuple-element.208), channel_id=1, source_target_pairs={{0,12},{1,13},{2,14},{3,15},{4,8},{5,9},{6,10},{7,11},{8,4},{9,5},... | collective-permute-start | bytes 1769480 | tf_op jit(solution)/shard_map/ppermute | solution.py:68
  155.5 12.5 %collective-permute-start.13 = (bf16[2,384,384]{2,1,0:T(8,128)(2,1)}, bf16[2,384,384]{2,1,0:T(8,128)(2,1)S(1)}, u32[]{:S(2)}, u32[]{:S(2)}) collective-permute-start(bf16[2,384,384]{2,1,0:T(8,128)(2,1)} %get-tuple-element.209), channel_id=1, source_target_pairs={{0,96},{1,97},{2,98},{3,99},{4,100},{5,101},{6,102},{7,103},{8,104... | collective-permute-start | bytes 1769480 | tf_op jit(solution)/shard_map/ppermute | solution.py:68
  155.9 12.1 %collective-permute-start.14 = (bf16[2,384,384]{2,1,0:T(8,128)(2,1)}, bf16[2,384,384]{2,1,0:T(8,128)(2,1)}, u32[]{:S(2)}, u32[]{:S(2)}) collective-permute-start(bf16[2,384,384]{2,1,0:T(8,128)(2,1)} %get-tuple-element.210), channel_id=1, source_target_pairs={{0,3},{1,2},{2,1},{3,0},{4,7},{5,6},{6,5},{7,4},{8,11},{9,10},{10,... | collective-permute-start | bytes 1769480 | tf_op jit(solution)/shard_map/ppermute | solution.py:68
  156.2 26.5 %all-to-all-start.2 = ((bf16[8,384,384]{2,1,0:T(8,128)(2,1)}), bf16[8,384,384]{2,1,0:T(8,128)(2,1)S(1)}, u32[]{:S(2)}, u32[]{:S(2)}) async-start(bf16[8,384,384]{2,1,0:T(8,128)(2,1)} %get-tuple-element.225), calls=%async_computation.2 | async-start | bytes 4718592 | tf_op jit(solution)/shard_map/all_to_all | solution.py:85
  159.8 62.4 %reduce-scatter.2.cloned.1.call-start = ((), (), s32[]{:S(2)}) async-start(), calls=%async_computation.5 | async-start | bytes 1769472 | tf_op jit(solution)/shard_map/reduce_scatter | solution.py:917
  173.1 8.8 %collective-permute-start.15 = (bf16[1,384,384]{2,1,0:T(8,128)(2,1)}, bf16[1,384,384]{2,1,0:T(8,128)(2,1)S(1)}, u32[]{:S(2)}, u32[]{:S(2)}) collective-permute-start(bf16[1,384,384]{2,1,0:T(8,128)(2,1)} %get-tuple-element.220), channel_id=1, source_target_pairs={{0,96},{1,97},{2,98},{3,99},{4,100},{5,101},{6,102},{7,103},{8,104... | collective-permute-start | bytes 884744 | tf_op jit(solution)/shard_map/ppermute | solution.py:68
  174.2 8.5 %collective-permute-start.16 = (bf16[1,384,384]{2,1,0:T(8,128)(2,1)}, bf16[1,384,384]{2,1,0:T(8,128)(2,1)S(1)}, u32[]{:S(2)}, u32[]{:S(2)}) collective-permute-start(bf16[1,384,384]{2,1,0:T(8,128)(2,1)} %get-tuple-element.222), channel_id=1, source_target_pairs={{0,3},{1,2},{2,1},{3,0},{4,7},{5,6},{6,5},{7,4},{8,11},{9,10},{10,... | collective-permute-start | bytes 884744 | tf_op jit(solution)/shard_map/ppermute | solution.py:68
  175.4 7.3 %collective-permute-start.17 = (bf16[1,384,384]{2,1,0:T(8,128)(2,1)}, bf16[1,384,384]{2,1,0:T(8,128)(2,1)S(1)}, u32[]{:S(2)}, u32[]{:S(2)}) collective-permute-start(bf16[1,384,384]{2,1,0:T(8,128)(2,1)} %get-tuple-element.224), channel_id=1, source_target_pairs={{0,12},{1,13},{2,14},{3,15},{4,8},{5,9},{6,10},{7,11},{8,4},{9,5},... | collective-permute-start | bytes 884744 | tf_op jit(solution)/shard_map/ppermute | solution.py:68
  188.5 19.8 %copy-start.1 = (s32[2]{0:T(128)S(1)}, s32[2]{0:T(128)}, u32[]{:S(2)}) copy-start(s32[2]{0:T(128)} %pad_add_fusion.1.scal) | copy-start | bytes 28
  209.8 12.4 %collective-permute-start.18 = (f32[15,8,384]{2,1,0:T(8,128)S(1)}, f32[15,8,384]{2,1,0:T(8,128)S(1)}, u32[]{:S(2)}, u32[]{:S(2)}) collective-permute-start(f32[15,8,384]{2,1,0:T(8,128)S(1)} %get-tuple-element.227), channel_id=1, source_target_pairs={{0,16},{1,17},{2,18},{3,19},{4,20},{5,21},{6,22},{7,23},{8,24},{9,... | collective-permute-start | bytes 552968 | tf_op jit(solution)/shard_map/ppermute | solution.py:68
  (13 other events, 12.0 us)
Sparse Core Ops, SparseCore 0:
  14.6 95.4 all-gather.2
  168.2 51.5 reduce-scatter.1
where the time goes:
time: 234 us
  Pallas kernels  82.9 us (35%)
  waiting for transfers between devices  50.5 us (22%)
  starting transfers between devices  47.1 us (20%)
  blocking collectives  19.8 us (8%)
  between operations  14.4 us (6%)
  local copies, waits for them, and re-layouts  11.1 us (5%)
  other arithmetic  7.77 us (3%)
    ppermute x19, waiting for transfers between devices, permute(): return lax.ppermute(value, AXES, pairs)  44.4 us
    pallas_call x9, Pallas kernels, call(): pl.pallas_call(kernel, out_shape=out_shape, in_specs=specs, out_specs=jax...  33.8 us
    ppermute x19, starting transfers between devices, permute(): return lax.ppermute(value, AXES, pairs)  27.6 us
    all_to_all x1, blocking collectives, exchange(): lax.all_to_all(blocks, AXES, 0, 0, tiled=True, axis_index_groups=cube_gro...  19.8 us
    all_to_all x3, starting transfers between devices, exchange(): lax.all_to_all(blocks, AXES, 0, 0, tiled=True, axis_index_groups=cube_gro...  19.2 us
    pallas_call x1, Pallas kernels, shards(): pl.pallas_call(ffn_kernel, out_shape=ffn_out, grid=(4,), in_specs=[scalar...  17.2 us
    pallas_call x1, Pallas kernels, shards(): pl.pallas_call(attn_backward_kernel, out_shape=(shape((2, 128, D), F32),...  14.5 us
    pallas_call x2, Pallas kernels, next_terms(): pl.pallas_call(terms_kernel, out_shape=(shape((count // 2, HALF, HALF), B...  9.49 us
  transfers between devices with their start and end apart: 24, of which 14 were waited for; matrix products, arithmetic and copies ran while one was open for 5% of the time, Pallas kernels for 23%

commit v1 on v0

--- a/solution.py
+++ b/solution.py
@@ -100,18 +100,12 @@
     return jnp.stack(rows).astype(jnp.int32)
 
 
-def spread_matrix():
-    place = jnp.arange(512, dtype=jnp.int32)
-    chip, core, row = place // 16, (place // 8) % 2, place % 8
-    wanted = jnp.where(row < 6, ((chip // 16 * 2 + core) * 16 + chip % 16) * 6 + row, -1)
-    return (lax.broadcasted_iota(jnp.int32, (HALF, 512), 0) == wanted[None, :]).astype(BF)
-
-
 def placed_features(chips):
+    chips = jnp.concatenate([chips, jnp.arange(64, dtype=jnp.int32)[None, :]], axis=0)
     row = jnp.arange(12, dtype=jnp.int32)[None, None, :]
     chip = chips[:, :, None]
     wanted = (((chip // 16) * 2 + row // 6) * 16 + chip % 16) * 6 + row % 6
-    return jnp.pad(wanted.reshape(4, D), ((0, 4), (0, 0)))
+    return jnp.pad(wanted.reshape(5, D), ((0, 3), (0, 0)))
 
 
 def placed_matrix(wanted):
@@ -181,11 +175,16 @@
 
 
 def merge_ffn_kernel(scal, keep, other, wd, ffn):
-    for k in range(8):
-        ffn[k] = both_cores(scal[1], keep[k], other[k])
+    to = lax.broadcasted_iota(jnp.int32, (48, 64), 0)
+    at = lax.broadcasted_iota(jnp.int32, (48, 64), 1)
+    row = to % 12
+    pick = (at == (to // 12) * 16 + (row // 6) * 8 + row % 6).astype(BF)
+    for w in range(2):
+        blocks = [both_cores(scal[1], keep[4 * w + k], other[4 * w + k]) for k in range(4)]
+        ffn[48 * w : 48 * w + 48, :] = dot(pick, jnp.concatenate(blocks, axis=0)).astype(BF)
     for j in range(3):
         rows = wd[8 * j : 8 * j + 8, :]
-        ffn[8 + j] = jnp.concatenate([rows[:, :HALF], rows[:, HALF:]], axis=0).astype(BF)
+        ffn[96 + 16 * j : 112 + 16 * j, :] = jnp.concatenate([rows[:, :HALF], rows[:, HALF:]], axis=0).astype(BF)
 
 
 def merge_attn_kernel(scal, keep, other, attn):
@@ -316,13 +315,10 @@
     cot,
     cot_other,
     wanted,
-    e2,
     g2,
     wg,
     wu,
-    wd0,
-    wd1,
-    wd2,
+    wd,
     out_keep,
     dh2_out,
     resid,
@@ -332,6 +328,8 @@
     send_u,
     keep_d,
     send_d,
+    pn,
+    dense,
     h2p,
     h2p_t,
     dy,
@@ -348,8 +346,15 @@
         resid[...] = r
         scale = lax.rsqrt(jnp.mean(r * r, axis=1, keepdims=True) + EPS)
         h2 = (r * scale * g2[0:1, :]).astype(BF)
-        h2p[:, :512] = dot(h2[:, :HALF], e2[...]).astype(BF)
-        h2p[:, 512:] = dot(h2[:, HALF:], e2[...]).astype(BF)
+        pn[...] = placed_matrix(wanted[4:5, :])
+        to = lax.broadcasted_iota(jnp.int32, (HALF, HALF), 0)
+        at = (to % 96 // 12) * 48 + 12 * (to // 96) + to % 12
+        pick = (lax.broadcasted_iota(jnp.int32, (HALF, HALF), 1) == at).astype(BF)
+        for k, w in ((0, wg), (1, wu)):
+            for q in range(8):
+                rows = dot(pick, w[8 * q : 8 * q + 8].reshape(HALF, HALF)).astype(BF)
+                dense[k, :, 96 * q : 96 * q + 96, :] = rows.reshape(4, 96, HALF)
+        h2p[...] = dot(h2, pn[...]).astype(BF)
         for k in range(2):
             h2p_t[k] = dot(h2, placed_matrix(wanted[k : k + 1, :])).astype(BF).T
         dy[pl.ds(pl.multiple_of(core * 128, 128), 128), :] = cot[...]
@@ -357,9 +362,9 @@
         acc_out[...] = jnp.zeros_like(acc_out)
         acc_dh2[...] = jnp.zeros_like(acc_dh2)
 
-    w_gate, w_up = wg[...].reshape(1024, HALF), wu[...].reshape(1024, HALF)
+    w_gate, w_up = dense[0, j], dense[1, j]
     gate, up = dot(h2p[...], w_gate), dot(h2p[...], w_up)
-    blocks = jnp.concatenate([wd0[...], wd1[...], wd2[...]], axis=1).astype(F32)
+    blocks = wd[...].reshape(16, 3, 16, HALF).astype(F32)
     w_down = jnp.concatenate(
         [blocks[:, :, 0:8, :].reshape(HALF, HALF), blocks[:, :, 8:16, :].reshape(HALF, HALF)], axis=1
     ).astype(BF)
@@ -382,9 +387,7 @@
         mine = pl.multiple_of(core * 128, 128)
         other = pl.multiple_of((1 - core) * 128, 128)
         out_keep[...] = acc_out[pl.ds(mine, 128), :]
-        dh2 = acc_dh2[...].astype(BF)
-        dh2_out[:TOK, :HALF] = dot_nt(dh2[:, :512], e2[...]).astype(BF)
-        dh2_out[:TOK, HALF:] = dot_nt(dh2[:, 512:], e2[...]).astype(BF)
+        dh2_out[:TOK, :] = dot_nt(acc_dh2[...].astype(BF), pn[...]).astype(BF)
         dh2_out[TOK:, :] = acc_out[pl.ds(other, 128), :].astype(BF)
 
         def write(w, carry):
@@ -415,9 +418,9 @@
     q,
     k_all,
     v_all,
-    h_t,
-    cosine,
-    sine,
+    h_t_in,
+    cosine_in,
+    sine_in,
     dres_out,
     dq_out,
     dk_out,
@@ -427,13 +430,23 @@
     inner,
     grad_o,
     pa,
+    h_t,
+    cosine,
+    sine,
+    sems,
 ):
     core = scal[1]
     own = pl.ds(pl.multiple_of(scal[0] * TOK, TOK), TOK)
     step = pl.program_id(0)
+    copies = [
+        pltpu.make_async_copy(source, target, sems.at[k])
+        for k, (source, target) in enumerate(((h_t_in, h_t), (cosine_in, cosine), (sine_in, sine)))
+    ]
 
     @pl.when(step == 0)
     def _():
+        for copy in copies:
+            copy.start()
         pa[...] = placed_matrix(wanted[3:4, :])
         r = resid[...]
         dh2 = dh2_a[...].astype(F32) + dh2_b[...].astype(F32)
@@ -467,6 +480,11 @@
         dres_out[0] = dres[0:128, :]
         dres_out[1] = dres[128:256, :]
 
+    @pl.when(step == 1)
+    def _():
+        for copy in copies:
+            copy.wait()
+
     @pl.when(step > 0)
     def _():
         t = step - 1
@@ -496,15 +514,18 @@
         grads[:, 288:384, :] = grad_o[t]
 
 
-def dh1_kernel(scal, dq, dk, dv, attn, wanted, out, pa):
+def dh1_kernel(scal, dq, dk, dv, attn, wanted, out, pa, total):
     @pl.when(pl.program_id(0) == 0)
     def _():
         pa[...] = placed_matrix(wanted[3:4, :])
 
-    wq, wk, wv = (weight_at(attn, k) for k in range(3))
-    mine = jnp.where(scal[0] == pl.program_id(0), dq[...], jnp.zeros_like(dq))
-    total = dot_nt(dk[...], wk) + dot_nt(dv[...], wv) + dot_nt(mine, wq)
-    out[...] = dot_nt(total.astype(BF), pa[...]).astype(BF)
+    total[...] = dot_nt(dk[...], weight_at(attn, 1)) + dot_nt(dv[...], weight_at(attn, 2))
+
+    @pl.when(scal[0] == pl.program_id(0))
+    def _():
+        total[...] += dot_nt(dq[...], weight_at(attn, 0))
+
+    out[...] = dot_nt(total[...].astype(BF), pa[...]).astype(BF)
 
 
 def terms_kernel(*refs):
@@ -655,7 +676,7 @@
 
 
 def next_terms(keeps, got):
-    count, rows = keeps[0].shape[0], 96
+    count, rows = keeps[0].shape[0], 192
     pair = [pl.BlockSpec((count // 2, rows, HALF), lambda j: (0, j, 0))] * 6
     out = pl.pallas_call(
         terms_kernel,
@@ -663,7 +684,7 @@
         grid=(HALF // rows,),
         in_specs=[pl.BlockSpec((count, rows, HALF), lambda j: (0, j, 0))] * 6,
         out_specs=tuple(pair),
-        compiler_params=params(),
+        compiler_params=params(54),
         cost_estimate=cost(1),
         name="next_terms",
     )(*(v for pair in zip(keeps, got) for v in pair))
@@ -696,9 +717,10 @@
     keep, send = call(pack_ffn_kernel, (halves, halves), (scal, wg, wu), name="pack_feed_forward")
     ffn_w = call(
         merge_ffn_kernel,
-        shape((11, 16, HALF), BF),
+        shape((144, HALF), BF),
         (scal, keep, permute(send, CORE_PAIRS), wd),
         name="merge_feed_forward",
+        mib=56,
     )
     ffn_w, wq, wk, wv, wo, gains, inputs, doc_ids, cotangent = lax.optimization_barrier(
         (ffn_w, wq, wk, wv, wo, gains, inputs, doc_ids, cotangent)
@@ -714,16 +736,15 @@
     )
     theirs, cot_other = permute(send, CORE_PAIRS), permute(cotangent[0], CORE_PAIRS)
     theirs, cot_other = lax.optimization_barrier((theirs, cot_other))
-    attn = call(merge_attn_kernel, shape((8, 5, 16, HALF), BF), (scal, keep, theirs), name="merge_attention")
+    attn = call(merge_attn_kernel, shape((8, 5, 16, HALF), BF), (scal, keep, theirs), name="merge_attention", mib=56)
 
     ids_row = jnp.zeros((16, D), BF).at[0, :128].set(doc_ids[0].astype(BF))
     block = jnp.concatenate([inputs[0], ids_row], axis=0)
     attn, block = lax.optimization_barrier((attn, block))
     attn = exchange(attn, 1)
     seq = [block, flipped(block, 1), flipped(block, 3)]
-    e2 = spread_matrix()
     wanted = placed_features(chips)
-    attn, wanted, chips, e2 = lax.optimization_barrier((attn, wanted, chips, e2))
+    attn, wanted, chips = lax.optimization_barrier((attn, wanted, chips))
     attn = call(dense_kernel, shape((8, 512, HALF), BF), (attn,), smem=0, name="dense_rows", mib=16)
     attn = exchange(attn, 3)
     seq.append(flipped(seq[1], 3))
@@ -758,6 +779,7 @@
         (scal, seq, seq_other, cosine, sine, start_row, wanted, attn),
         scratch=(pltpu.VMEM((LEN, D), BF), pltpu.VMEM((LEN, TOK), F32), pltpu.VMEM((D, D), BF)),
         name="attention_forward",
+        mib=54,
         micros=1.3e7,
     )
     po_other = permute(po, CORE_PAIRS)
@@ -784,21 +806,22 @@
             full((128, D)),
             full((128, D)),
             full((8, D)),
-            full((HALF, 512)),
             full((8, D)),
-            pl.BlockSpec((64, 1, 16, HALF), lambda j: (0, j, 0, 0)),
-            pl.BlockSpec((64, 1, 16, HALF), lambda j: (0, 4 + j, 0, 0)),
-            *(pl.BlockSpec((16, 1, 16, HALF), lambda j, k=k: (j, 8 + k, 0, 0)) for k in range(3)),
+            pl.BlockSpec((64, 48, HALF), lambda j: (0, 0, 0)),
+            pl.BlockSpec((64, 48, HALF), lambda j: (0, 1, 0)),
+            pl.BlockSpec((16, 48, HALF), lambda j: (j, 2, 0)),
         ],
         out_specs=tuple(full(s.shape) for s in ffn_out[:3])
         + (column,) * 4
         + tuple(full(s.shape) for s in ffn_out[7:]),
         scratch_shapes=[
-            pltpu.VMEM((TOK, 1024), BF),
+            pltpu.VMEM((D, D), BF),
+            pltpu.VMEM((2, 4, D, HALF), BF),
+            pltpu.VMEM((TOK, D), BF),
             pltpu.VMEM((2, D, TOK), BF),
             pltpu.VMEM((TOK, D), BF),
             pltpu.VMEM((TOK, D), F32),
-            pltpu.VMEM((TOK, 1024), F32),
+            pltpu.VMEM((TOK, D), F32),
             pltpu.VMEM((FF // 2, D), F32),
         ],
         compiler_params=params(),
@@ -813,9 +836,8 @@
         cotangent[0],
         cot_other,
         wanted,
-        e2,
         g2,
-        *((ffn_w,) * 5),
+        *((ffn_w,) * 3),
     )
 
     dh2_other = permute(dh2, CORE_PAIRS)
@@ -850,9 +872,7 @@
             short,
             long,
             long,
-            full((D, LEN)),
-            full((LEN, 128)),
-            full((LEN, 128)),
+            *([pl.BlockSpec(memory_space=pl.ANY)] * 3),
         ],
         out_specs=(
             full((2, 128, D)),
@@ -866,6 +886,10 @@
             pltpu.VMEM((8, TOK), F32),
             pltpu.VMEM((3, 8, 96, 128), BF),
             pltpu.VMEM((D, D), BF),
+            pltpu.VMEM((D, LEN), BF),
+            pltpu.VMEM((LEN, 128), F32),
+            pltpu.VMEM((LEN, 128), F32),
+            pltpu.SemaphoreType.DMA((3,)),
         ],
         compiler_params=params(),
         cost_estimate=cost(1),
@@ -893,8 +917,9 @@
     )
     parts = [(kg, sg), (ku, su), (kd.reshape(4, HALF, HALF), sd.reshape(4, HALF, HALF))]
     got = first_terms(parts)
+    exchanged = exchange(grads, 3)
     grads, dq, dk, dv, got = lax.optimization_barrier((grads, dq, dk, dv, got))
-    grads = exchange(grads, 3)
+    grads = exchanged
     dh1 = pl.pallas_call(
         dh1_kernel,
         out_shape=shape((LEN, D), BF),
@@ -908,14 +933,14 @@
             full((8, D)),
         ],
         out_specs=pl.BlockSpec((TOK, D), lambda b: (b, 0)),
-        scratch_shapes=[pltpu.VMEM((D, D), BF)],
+        scratch_shapes=[pltpu.VMEM((D, D), BF), pltpu.VMEM((TOK, D), F32)],
         compiler_params=params(),
         cost_estimate=cost(1),
         name="attention_input_gradient",
     )(scal, dq, dk, dv, attn, wanted)
     terms, dh1 = reduce_rows(parts, got, dh1)
     dh1 = lax.psum_scatter(dh1, ("z", "core"), scatter_dimension=0, tiled=True)
-    blocks = call(padded_kernel, shape((8, 15, 16, HALF), BF), (*terms, grads), smem=0, name="padded_rows")
+    blocks = call(padded_kernel, shape((8, 15, 16, HALF), BF), (*terms, grads), smem=0, name="padded_rows", mib=54)
     blocks = exchange(blocks, 1)
 
     grads, theirs = call(
@@ -928,6 +953,7 @@
         shapes * 3 + tuple(shape(m.shape, BF) for m in masters) + (shape((128, D), BF), shape((128, D), F32)),
         (scal, grads, theirs, inputs[0], dh1, g1, dres, resid, out_keep, dh2_other, *masters, *moments, *averages),
         name="update",
+        mib=56,
     )
     outs, output, input_grad = outs[:32], *outs[32:]
     outs = tuple(v.T if k % 8 == 7 else v for k, v in enumerate(outs))

time: 234 us -> 231 us (0.987)
  waiting for transfers between devices: 50.5 us -> 46.4 us
    ppermute x19, waiting for transfers between devices: 44.4 us -> 40.6 us  [permute(): return lax.ppermute(value, AXES, pairs)]
    all_gather x1, waiting for transfers between devices: 3.18 us -> 0.01 us  [shards(): ffn_w = lax.all_gather(ffn_w, ('z', 'y', 'x'), axis=0, tiled=False)]
    all_to_all x3, waiting for transfers between devices: 2.92 us -> 5.84 us  [exchange(): lax.all_to_all(blocks, AXES, 0, 0, tiled=True, axis_index_groups=cube_gro...]
    pallas_call x1, Pallas kernels: 17.2 us -> 20 us  [shards(): pl.pallas_call(ffn_kernel, out_shape=ffn_out, grid=(4,), in_specs=[scalar...]
    unnamed x44 -> x40, local copies, waits for them, and re-layouts: 7.32 us -> 7.49 us
  transfers between devices with their start and end apart: 24 -> 24, of which waited for: 14 -> 15; matrix products, arithmetic and copies ran while one was open for 5% -> 5% of each run, Pallas kernels for 23% -> 22%
where the time goes in v1:
time: 231 us; the launch traced here: 230 us
  Pallas kernels  83.2 us (36%)
  waiting for transfers between devices  46.4 us (20%)
  starting transfers between devices  45.9 us (20%)
  blocking collectives  19.9 us (9%)
  between operations  14.4 us (6%)
  local copies, waits for them, and re-layouts  11.3 us (5%)
  other arithmetic  9.18 us (4%)
    ppermute x19, waiting for transfers between devices, permute(): return lax.ppermute(value, AXES, pairs)  40.6 us
    pallas_call x9, Pallas kernels, call(): pl.pallas_call(kernel, out_shape=out_shape, in_specs=specs, out_specs=jax...  34.1 us
    ppermute x19, starting transfers between devices, permute(): return lax.ppermute(value, AXES, pairs)  26 us
    pallas_call x1, Pallas kernels, shards(): pl.pallas_call(ffn_kernel, out_shape=ffn_out, grid=(4,), in_specs=[scalar...  20 us
    all_to_all x1, blocking collectives, exchange(): lax.all_to_all(blocks, AXES, 0, 0, tiled=True, axis_index_groups=cube_gro...  19.9 us
    all_to_all x3, starting transfers between devices, exchange(): lax.all_to_all(blocks, AXES, 0, 0, tiled=True, axis_index_groups=cube_gro...  19.8 us
    pallas_call x1, Pallas kernels, shards(): pl.pallas_call(attn_backward_kernel, out_shape=(shape((2, 128, D), F32),...  13.7 us
    pallas_call x2, Pallas kernels, next_terms(): pl.pallas_call(terms_kernel, out_shape=(shape((count // 2, HALF, HALF), B...  7.73 us
  transfers between devices with their start and end apart: 24, of which 15 were waited for; matrix products, arithmetic and copies ran while one was open for 5% of the time, Pallas kernels for 22%

profile of v1, /device:TPU:1, one launch (start us, length us, event | category | flops | bytes accessed | tf_op | source)
XLA Modules:
  0.0 230.4 jit_solution(14725613423432803186)
XLA Ops:
  7.9 1.6 pack_feed_forward.1
  9.6 1.4 collective-permute-start
  12.8 1.8 merge_feed_forward.1
  16.8 1.5 pack_attention.1
  21.0 1.7 merge_attention.1
  22.8 11.9 %all-to-all-start = ((bf16[8,5,16,384]{3,2,1,0:T(8,128)(2,1)}), bf16[8,5,16,384]{3,2,1,0:T(8,128)(2,1)S(1)}, u32[]{:S(2)}, u32[]{:S(2)}) async-start(bf16[8,5,16,384]{3,2,1,0:T(8,128)(2,1)} %merge_attention.1), calls=%async_computation | async-start | bytes 983040 | tf_op jit(solution)/shard_map/all_to_all | solution.py:85
  36.5 2.5 %all-to-all-done.blocks = bf16[8,5,16,384]{3,2,1,0:T(8,128)(2,1)S(1)} async-done(((bf16[8,5,16,384]{3,2,1,0:T(8,128)(2,1)}), bf16[8,5,16,384]{3,2,1,0:T(8,128)(2,1)S(1)}, u32[]{:S(2)}, u32[]{:S(2)}) %all-to-all-start) | async-done | bytes 491552 | tf_op jit(solution)/shard_map/all_to_all | solution.py:85
  39.0 2.2 dense_rows.1
  41.2 3.6 %all-to-all-start.1 = ((bf16[8,512,384]{2,1,0:T(8,128)(2,1)}), bf16[8,512,384]{2,1,0:T(8,128)(2,1)S(1)}, u32[]{:S(2)}, u32[]{:S(2)}) async-start(bf16[8,512,384]{2,1,0:T(8,128)(2,1)} %dense_rows.1), calls=%async_computation.1 | async-start | bytes 6291456 | tf_op jit(solution)/shard_map/all_to_all | solution.py:85
  44.9 2.4 %collective-permute-start.3 = (bf16[144,768]{1,0:T(8,128)(2,1)S(1)}, bf16[144,768]{1,0:T(8,128)(2,1)S(1)}, u32[]{:S(2)}, u32[]{:S(2)}) collective-permute-start(bf16[144,768]{1,0:T(8,128)(2,1)S(1)} %fusion.2), channel_id=1, source_target_pairs={{0,32},{1,33},{2,34},{3,35},{4,36},{5,37},{6,38},{7,39},{8,40},{9,... | collective-permute-start | bytes 663560 | tf_op jit(solution)/shard_map/ppermute | solution.py:68
  48.0 6.3 %collective-permute-done.3 = bf16[144,768]{1,0:T(8,128)(2,1)S(1)} collective-permute-done((bf16[144,768]{1,0:T(8,128)(2,1)S(1)}, bf16[144,768]{1,0:T(8,128)(2,1)S(1)}, u32[]{:S(2)}, u32[]{:S(2)}) %collective-permute-start.3) | collective-permute-done | bytes 221216 | tf_op jit(solution)/shard_map/ppermute | solution.py:68
  55.2 19.0 %collective-permute-done.4 = bf16[144,768]{1,0:T(8,128)(2,1)S(1)} collective-permute-done((bf16[144,768]{1,0:T(8,128)(2,1)S(1)}, bf16[144,768]{1,0:T(8,128)(2,1)S(1)}, u32[]{:S(2)}, u32[]{:S(2)}) %collective-permute-start.4) | collective-permute-done | bytes 221216 | tf_op jit(solution)/shard_map/ppermute | solution.py:68
  74.2 2.3 collective-permute-done.5
  77.5 1.6 collective-permute-start.6
  82.8 3.1 %fusion = (f32[1024,128]{1,0:T(8,128)}, f32[1024,128]{1,0:T(8,128)}) fusion(f32[128]{0:T(128)S(1)} %mul.184, f32[128]{0:T(128)S(1)} %mul.181, f32[1024]{0:T(1024)S(1)} %get-tuple-element.265), kind=kLoop, calls=%fused_computation.4 | loop fusion | flops 262144 | bytes 1053696 | tf_op jit(solution)/shard_map/mul | solution.py:762
  87.7 16.4 %attention_forward.1 = (bf16[256,384]{1,0:T(8,128)(2,1)}, bf16[1024,384]{1,0:T(8,128)(2,1)}, bf16[1024,384]{1,0:T(8,128)(2,1)}, bf16[1024,768]{1,0:T(8,128)(2,1)...) custom-call(s32[2]{0:T(128)} %pad_add_fusion.1.scal, ...), custom_call_target="tpu_custom_call" | custom-call | flops 13000000512 | bytes 1 | tf_op jit(solution)/shard_map/attention_forward/pallas_call | solution.py:650
  104.4 1.9 collective-permute-done.7.part_b.o_other
  107.1 20.0 %feed_forward.1 = (f32[128,768]{1,0:T(8,128)}, bf16[384,768]{1,0:T(8,128)(2,1)}, f32[256,768]{1,0:T(8,128)}, bf16[4,384,384]{2,1,0:T(8,128)(2,1)}, bf16[4,384,38...) custom-call(s32[2]{0:T(128)} %pad_add_fusion.1.scal, ...), custom_call_target="tpu_custom_call" | custom-call | flops 4001 | bytes 1 | tf_op jit(solution)/shard_map/feed_forward/pallas_call | solution.py:796
  127.6 1.9 collective-permute-done.8.dh2_b.out_b
  131.9 13.7 %attention_backward.1 = (f32[2,128,768]{2,1,0:T(8,128)}, bf16[256,384]{1,0:T(8,128)(2,1)}, bf16[1024,384]{1,0:T(8,128)(2,1)}, bf16[1024,384]{1,0:T(8,128)(2,1)}, bf16[8,384,384]{2,1,0:T(8,128)(2,1)}) custom-call(s32[2]{0:T(128)} %pad_add_fusion.1.scal, f32[256,768]{1,0:T(8,128)} %get-tuple-element.185.resid, bf16[384,768]{1,0:T(8,128)(2,1)} %get-tuple-element.177.dh2_a, ...), custom_call_target="tpu_custom_call" | custom-call | flops 1001 | bytes 1 | tf_op jit(solution)/shard_map/attention_backward/pallas_call | solution.py:848
  148.5 4.7 %next_terms.2 = (bf16[2,384,384]{2,1,0:T(8,128)(2,1)}, bf16[2,384,384]{2,1,0:T(8,128)(2,1)}, bf16[2,384,384]{2,1,0:T(8,128)(2,1)}, bf16[2,384,384]{2,1,0:T(8,128...) custom-call(bf16[4,384,384]{2,1,0:T(8,128)(2,1)} %get-tuple-element.184.refs_0_, ...), custom_call_target="tpu_custom_call" | custom-call | flops 1001 | bytes 1 | tf_op jit(solution)/shard_map/next_terms/pallas_call | solution.py:681
  154.1 4.2 %all-to-all-start.2 = ((bf16[8,384,384]{2,1,0:T(8,128)(2,1)}), bf16[8,384,384]{2,1,0:T(8,128)(2,1)S(1)}, u32[]{:S(2)}, u32[]{:S(2)}) async-start(bf16[8,384,384]{2,1,0:T(8,128)(2,1)} %get-tuple-element.192), calls=%async_computation.2 | async-start | bytes 4718592 | tf_op jit(solution)/shard_map/all_to_all | solution.py:85
  158.4 7.7 %attention_input_gradient.1 = bf16[1024,768]{1,0:T(8,128)(2,1)} custom-call(s32[2]{0:T(128)} %pad_add_fusion.1.scal, bf16[256,384]{1,0:T(8,128)(2,1)} %get-tuple-element.208.dq, bf16[1024,384]{1,0:T(8,128)(2,1)} %get-tuple-element.209.dk, bf16[1024,384]{1,0:T(8,128)(2,1)} %get-tuple-element.210.dv, bf16[8,512,384]{2,1,0:T(8,128)(2,1)} %copy-done.2, ...), custom_call_target="tpu_custom_call" | custom-call | flops 1001 | bytes 1 | tf_op jit(solution)/shard_map/attention_input_gradient/pallas_call | solution.py:923
  167.2 3.0 %next_terms.3 = (bf16[1,384,384]{2,1,0:T(8,128)(2,1)}, bf16[1,384,384]{2,1,0:T(8,128)(2,1)}, bf16[1,384,384]{2,1,0:T(8,128)(2,1)}, bf16[1,384,384]{2,1,0:T(8,128...) custom-call(bf16[2,384,384]{2,1,0:T(8,128)(2,1)} %get-tuple-element.204.refs_0_, ...), custom_call_target="tpu_custom_call" | custom-call | flops 1001 | bytes 1 | tf_op jit(solution)/shard_map/next_terms/pallas_call | solution.py:681
  170.2 1.5 collective-permute-start.15
  174.1 3.4 %all-to-all-done.2.attn = bf16[8,384,384]{2,1,0:T(8,128)(2,1)S(1)} async-done(((bf16[8,384,384]{2,1,0:T(8,128)(2,1)}), bf16[8,384,384]{2,1,0:T(8,128)(2,1)S(1)}, u32[]{:S(2)}, u32[]{:S(2)}) %all-to-all-start.2) | async-done | bytes 2359328 | tf_op jit(solution)/shard_map/all_to_all | solution.py:85
  177.5 2.1 collective-permute-done.15.y0
  179.5 1.6 collective-permute-done.16.y1
  182.0 4.2 %padded_rows.1 = bf16[8,15,16,384]{3,2,1,0:T(8,128)(2,1)} custom-call(bf16[1,384,384]{2,1,0:T(8,128)(2,1)} %get-tuple-element.216.x0, bf16[1,384,384]{2,1,0:T(8,128)(2,1)} %copy-done.12, bf16[1,384,384]{2,1,0:T(8,128)(2,1)} %get-tuple-element.218.x1, bf16[1,384,384]{2,1,0:T(8,128)(2,1)} %copy-done.13, bf16[1,384,384]{2,1,0:T(8,128)(2,1)} %get-tuple-element.220.x2, ...), custom_call_target="tpu_custom_call" | custom-call | flops 1001 | bytes 1 | tf_op jit(solution)/shard_map/padded_rows/pallas_call | solution.py:650
  186.2 19.9 %all_to_all.20.blocks = bf16[8,15,16,384]{3,2,1,0:T(8,128)(2,1)S(1)} all-to-all(bf16[8,15,16,384]{3,2,1,0:T(8,128)(2,1)} %padded_rows.1), channel_id=1, replica_groups={{0,1,4,5,32,33,36,37},{2,3,6,7,34,35,38,39},{8,9,12,13,40,41,44,45},{10..., dimensions={0} | all-to-all | bytes 2949120 | tf_op jit(solution)/shard_map/all_to_all | solution.py:85
  207.5 10.4 %collective-permute-start.18 = (f32[15,8,384]{2,1,0:T(8,128)S(1)}, f32[15,8,384]{2,1,0:T(8,128)S(1)}, u32[]{:S(2)}, u32[]{:S(2)}) collective-permute-start(f32[15,8,384]{2,1,0:T(8,128)S(1)} %get-tuple-element.223), channel_id=1, source_target_pairs={{0,16},{1,17},{2,18},{3,19},{4,20},{5,21},{6,22},{7,23},{8,24},{9,... | collective-permute-start | bytes 552968 | tf_op jit(solution)/shard_map/ppermute | solution.py:68
  219.7 3.8 %update.1 = (f32[6,768]{1,0:T(8,128)}, f32[6,768]{1,0:T(8,128)}, f32[6,768]{1,0:T(8,128)}, f32[6,768]{1,0:T(8,128)}, f32[6,3072]{1,0:T(8,128)}, /*index=5*/f32[6...) custom-call(s32[2]{0:T(128)} %pad_add_fusion.1.scal, ...), custom_call_target="tpu_custom_call" | custom-call | flops 1001 | bytes 1 | tf_op jit(solution)/shard_map/update/pallas_call | solution.py:650
  (112 shorter events, 32.7 us)
Async XLA Ops:
  7.2 99.1 %all-gather.3.cloned.1.call-start = ((), (), s32[]{:S(2)}) async-start(), calls=%async_computation.6 | async-start | bytes 7188480 | tf_op jit(solution)/shard_map/all_gather | solution.py:728
  9.6 2.6 %collective-permute-start = (f32[8,8,384]{2,1,0:T(8,128)}, f32[8,8,384]{2,1,0:T(8,128)S(1)}, u32[]{:S(2)}, u32[]{:S(2)}) collective-permute-start(f32[8,8,384]{2,1,0:T(8,128)} %get-tuple-element.155), channel_id=1, source_target_pairs={{0,16},{1,17},{2,18},{3,19},{4,20},{5,21},{6,22},{7,23},{8,24},{9,... | collective-permute-start | bytes 294920 | tf_op jit(solution)/shard_map/ppermute | solution.py:68
  16.2 4.2 %collective-permute-start.2 = (bf16[128,768]{1,0:T(8,128)(2,1)}, bf16[128,768]{1,0:T(8,128)(2,1)S(1)}, u32[]{:S(2)}, u32[]{:S(2)}) collective-permute-start(bf16[128,768]{1,0:T(8,128)(2,1)} %bitcast.48), channel_id=1, source_target_pairs={{0,16},{1,17},{2,18},{3,19},{4,20},{5,21},{6,22},{7,23},{8,24},{9,... | collective-permute-start | bytes 589832 | tf_op jit(solution)/shard_map/ppermute | solution.py:68
  18.9 1.5 collective-permute-start.1
  20.4 2.4 %copy-start.9 = (bf16[128,768]{1,0:T(8,128)(2,1)}, bf16[128,768]{1,0:T(8,128)(2,1)S(1)}, u32[]{:S(2)}) copy-start(bf16[128,768]{1,0:T(8,128)(2,1)S(1)} %collective-permute-done.2.cot_other) | copy-start | bytes 589828
  22.8 16.2 %all-to-all-start = ((bf16[8,5,16,384]{3,2,1,0:T(8,128)(2,1)}), bf16[8,5,16,384]{3,2,1,0:T(8,128)(2,1)S(1)}, u32[]{:S(2)}, u32[]{:S(2)}) async-start(bf16[8,5,16,384]{3,2,1,0:T(8,128)(2,1)} %merge_attention.1), calls=%async_computation | async-start | bytes 983040 | tf_op jit(solution)/shard_map/all_to_all | solution.py:85
  41.2 44.7 %all-to-all-start.1 = ((bf16[8,512,384]{2,1,0:T(8,128)(2,1)}), bf16[8,512,384]{2,1,0:T(8,128)(2,1)S(1)}, u32[]{:S(2)}, u32[]{:S(2)}) async-start(bf16[8,512,384]{2,1,0:T(8,128)(2,1)} %dense_rows.1), calls=%async_computation.1 | async-start | bytes 6291456 | tf_op jit(solution)/shard_map/all_to_all | solution.py:85
  44.9 34.2 %copy-start.18 = (f32[2]{0:T(128)S(1)}, f32[2]{0:T(128)}, u32[]{:S(2)}) copy-start(f32[2]{0:T(128)} %constant.273.clone) | copy-start | bytes 28
  44.9 9.4 %collective-permute-start.3 = (bf16[144,768]{1,0:T(8,128)(2,1)S(1)}, bf16[144,768]{1,0:T(8,128)(2,1)S(1)}, u32[]{:S(2)}, u32[]{:S(2)}) collective-permute-start(bf16[144,768]{1,0:T(8,128)(2,1)S(1)} %fusion.2), channel_id=1, source_target_pairs={{0,32},{1,33},{2,34},{3,35},{4,36},{5,37},{6,38},{7,39},{8,40},{9,... | collective-permute-start | bytes 663560 | tf_op jit(solution)/shard_map/ppermute | solution.py:68
  47.3 26.9 %collective-permute-start.4 = (bf16[144,768]{1,0:T(8,128)(2,1)S(1)}, bf16[144,768]{1,0:T(8,128)(2,1)S(1)}, u32[]{:S(2)}, u32[]{:S(2)}) collective-permute-start(bf16[144,768]{1,0:T(8,128)(2,1)S(1)} %fusion.2), channel_id=1, source_target_pairs={{0,96},{1,97},{2,98},{3,99},{4,100},{5,101},{6,102},{7,103},{8,104... | collective-permute-start | bytes 663560 | tf_op jit(solution)/shard_map/ppermute | solution.py:68
  54.3 22.2 %collective-permute-start.5 = (bf16[144,768]{1,0:T(8,128)(2,1)S(1)}, bf16[144,768]{1,0:T(8,128)(2,1)S(1)}, u32[]{:S(2)}, u32[]{:S(2)}) collective-permute-start(bf16[144,768]{1,0:T(8,128)(2,1)S(1)} %collective-permute-done.3), channel_id=1, source_target_pairs={{0,96},{1,97},{2,98},{3,99},{4,100},{5,101},{6,102},{7,103},{8,104... | collective-permute-start | bytes 663560 | tf_op jit(solution)/shard_map/ppermute | solution.py:68
  77.5 4.0 %collective-permute-start.6 = (bf16[4,144,768]{2,1,0:T(8,128)(2,1)}, bf16[4,144,768]{2,1,0:T(8,128)(2,1)}, u32[]{:S(2)}, u32[]{:S(2)}) collective-permute-start(bf16[4,144,768]{2,1,0:T(8,128)(2,1)} %pad_maximum_fusion.seq), channel_id=1, source_target_pairs={{0,16},{1,17},{2,18},{3,19},{4,20},{5,21},{6,22},{7,23},{8,24},{9,... | collective-permute-start | bytes 2654216 | tf_op jit(solution)/shard_map/ppermute | solution.py:68
  85.9 1.8 copy-start.2
  104.1 2.2 collective-permute-start.7
  127.1 2.3 collective-permute-start.8
  129.4 2.5 %copy-start.5 = (bf16[384,768]{1,0:T(8,128)(2,1)}, bf16[384,768]{1,0:T(8,128)(2,1)S(1)}, u32[]{:S(2)}) copy-start(bf16[384,768]{1,0:T(8,128)(2,1)S(1)} %collective-permute-done.8.dh2_b.out_b) | copy-start | bytes 1769476
  129.4 16.2 %collective-permute-start.9 = (bf16[4,384,384]{2,1,0:T(8,128)(2,1)}, bf16[4,384,384]{2,1,0:T(8,128)(2,1)S(1)}, u32[]{:S(2)}, u32[]{:S(2)}) collective-permute-start(bf16[4,384,384]{2,1,0:T(8,128)(2,1)} %get-tuple-element.196), channel_id=1, source_target_pairs={{0,3},{1,2},{2,1},{3,0},{4,7},{5,6},{6,5},{7,4},{8,11},{9,10},{10,... | collective-permute-start | bytes 3538952 | tf_op jit(solution)/shard_map/ppermute | solution.py:68
  130.7 15.6 %collective-permute-start.10 = (bf16[4,384,384]{2,1,0:T(8,128)(2,1)}, bf16[4,384,384]{2,1,0:T(8,128)(2,1)S(1)}, u32[]{:S(2)}, u32[]{:S(2)}) collective-permute-start(bf16[4,384,384]{2,1,0:T(8,128)(2,1)} %get-tuple-element.197), channel_id=1, source_target_pairs={{0,12},{1,13},{2,14},{3,15},{4,8},{5,9},{6,10},{7,11},{8,4},{9,5},... | collective-permute-start | bytes 3538952 | tf_op jit(solution)/shard_map/ppermute | solution.py:68
  131.9 15.6 %collective-permute-start.11 = (bf16[4,384,384]{2,1,0:T(8,128)(2,1)}, bf16[4,384,384]{2,1,0:T(8,128)(2,1)S(1)}, u32[]{:S(2)}, u32[]{:S(2)}) collective-permute-start(bf16[4,384,384]{2,1,0:T(8,128)(2,1)} %bitcast.63), channel_id=1, source_target_pairs={{0,96},{1,97},{2,98},{3,99},{4,100},{5,101},{6,102},{7,103},{8,104... | collective-permute-start | bytes 3538952 | tf_op jit(solution)/shard_map/ppermute | solution.py:68
  145.6 1.8 copy-start.6
  153.2 12.9 %collective-permute-start.12 = (bf16[2,384,384]{2,1,0:T(8,128)(2,1)}, bf16[2,384,384]{2,1,0:T(8,128)(2,1)S(1)}, u32[]{:S(2)}, u32[]{:S(2)}) collective-permute-start(bf16[2,384,384]{2,1,0:T(8,128)(2,1)} %get-tuple-element.205), channel_id=1, source_target_pairs={{0,12},{1,13},{2,14},{3,15},{4,8},{5,9},{6,10},{7,11},{8,4},{9,5},... | collective-permute-start | bytes 1769480 | tf_op jit(solution)/shard_map/ppermute | solution.py:68
  153.7 12.5 %collective-permute-start.13 = (bf16[2,384,384]{2,1,0:T(8,128)(2,1)}, bf16[2,384,384]{2,1,0:T(8,128)(2,1)S(1)}, u32[]{:S(2)}, u32[]{:S(2)}) collective-permute-start(bf16[2,384,384]{2,1,0:T(8,128)(2,1)} %get-tuple-element.206), channel_id=1, source_target_pairs={{0,96},{1,97},{2,98},{3,99},{4,100},{5,101},{6,102},{7,103},{8,104... | collective-permute-start | bytes 1769480 | tf_op jit(solution)/shard_map/ppermute | solution.py:68
  153.9 12.2 %collective-permute-start.14 = (bf16[2,384,384]{2,1,0:T(8,128)(2,1)}, bf16[2,384,384]{2,1,0:T(8,128)(2,1)}, u32[]{:S(2)}, u32[]{:S(2)}) collective-permute-start(bf16[2,384,384]{2,1,0:T(8,128)(2,1)} %get-tuple-element.207), channel_id=1, source_target_pairs={{0,3},{1,2},{2,1},{3,0},{4,7},{5,6},{6,5},{7,4},{8,11},{9,10},{10,... | collective-permute-start | bytes 1769480 | tf_op jit(solution)/shard_map/ppermute | solution.py:68
  154.1 23.3 %all-to-all-start.2 = ((bf16[8,384,384]{2,1,0:T(8,128)(2,1)}), bf16[8,384,384]{2,1,0:T(8,128)(2,1)S(1)}, u32[]{:S(2)}, u32[]{:S(2)}) async-start(bf16[8,384,384]{2,1,0:T(8,128)(2,1)} %get-tuple-element.192), calls=%async_computation.2 | async-start | bytes 4718592 | tf_op jit(solution)/shard_map/all_to_all | solution.py:85
  158.4 60.6 %reduce-scatter.2.cloned.1.call-start = ((), (), s32[]{:S(2)}) async-start(), calls=%async_computation.5 | async-start | bytes 1769472 | tf_op jit(solution)/shard_map/reduce_scatter | solution.py:942
  170.2 9.3 %collective-permute-start.15 = (bf16[1,384,384]{2,1,0:T(8,128)(2,1)}, bf16[1,384,384]{2,1,0:T(8,128)(2,1)S(1)}, u32[]{:S(2)}, u32[]{:S(2)}) collective-permute-start(bf16[1,384,384]{2,1,0:T(8,128)(2,1)} %get-tuple-element.217), channel_id=1, source_target_pairs={{0,96},{1,97},{2,98},{3,99},{4,100},{5,101},{6,102},{7,103},{8,104... | collective-permute-start | bytes 884744 | tf_op jit(solution)/shard_map/ppermute | solution.py:68
  171.7 9.5 %collective-permute-start.16 = (bf16[1,384,384]{2,1,0:T(8,128)(2,1)}, bf16[1,384,384]{2,1,0:T(8,128)(2,1)S(1)}, u32[]{:S(2)}, u32[]{:S(2)}) collective-permute-start(bf16[1,384,384]{2,1,0:T(8,128)(2,1)} %get-tuple-element.219), channel_id=1, source_target_pairs={{0,3},{1,2},{2,1},{3,0},{4,7},{5,6},{6,5},{7,4},{8,11},{9,10},{10,... | collective-permute-start | bytes 884744 | tf_op jit(solution)/shard_map/ppermute | solution.py:68
  172.9 8.3 %collective-permute-start.17 = (bf16[1,384,384]{2,1,0:T(8,128)(2,1)}, bf16[1,384,384]{2,1,0:T(8,128)(2,1)S(1)}, u32[]{:S(2)}, u32[]{:S(2)}) collective-permute-start(bf16[1,384,384]{2,1,0:T(8,128)(2,1)} %get-tuple-element.221), channel_id=1, source_target_pairs={{0,12},{1,13},{2,14},{3,15},{4,8},{5,9},{6,10},{7,11},{8,4},{9,5},... | collective-permute-start | bytes 884744 | tf_op jit(solution)/shard_map/ppermute | solution.py:68
  177.5 3.7 %copy-start.3 = (bf16[8,384,384]{2,1,0:T(8,128)(2,1)}, bf16[8,384,384]{2,1,0:T(8,128)(2,1)S(1)}, u32[]{:S(2)}) copy-start(bf16[8,384,384]{2,1,0:T(8,128)(2,1)S(1)} %all-to-all-done.2.attn) | copy-start | bytes 7077892
  179.5 1.6 copy-start.12
  186.2 19.9 %copy-start.1 = (s32[2]{0:T(128)S(1)}, s32[2]{0:T(128)}, u32[]{:S(2)}) copy-start(s32[2]{0:T(128)} %pad_add_fusion.1.scal) | copy-start | bytes 28
  207.5 11.4 %collective-permute-start.18 = (f32[15,8,384]{2,1,0:T(8,128)S(1)}, f32[15,8,384]{2,1,0:T(8,128)S(1)}, u32[]{:S(2)}, u32[]{:S(2)}) collective-permute-start(f32[15,8,384]{2,1,0:T(8,128)S(1)} %get-tuple-element.223), channel_id=1, source_target_pairs={{0,16},{1,17},{2,18},{3,19},{4,20},{5,21},{6,22},{7,23},{8,24},{9,... | collective-permute-start | bytes 552968 | tf_op jit(solution)/shard_map/ppermute | solution.py:68
  (11 other events, 9.2 us)
Sparse Core Ops, SparseCore 0:
  14.7 90.8 all-gather.2
  166.3 51.7 reduce-scatter.1

commit v2 on v1

--- a/solution.py
+++ b/solution.py
@@ -536,36 +536,38 @@
         refs[7 + 2 * k][...] = total[half:]
 
 
-def padded_kernel(x0, y0, x1, y1, x2, y2, attn, out):
-    pick = dense_rows()
-
-    def write(at, rows):
-        out[:, at] = dot_tn(pick, rows).astype(BF).reshape(8, 16, HALF)
-
-    for at, x, y in ((0, x0, y0), (4, x1, y1)):
-        total = (x[0].astype(F32) + y[0].astype(F32)).astype(BF)
-        for k in range(4):
-            write(at + k, total[96 * k : 96 * k + 96])
-    out[:, 12:15] = (x2[0].astype(F32) + y2[0].astype(F32)).astype(BF).reshape(8, 3, 16, HALF)
-    for k in range(4):
-        rows = slice(96 * k, 96 * k + 96)
-        total = attn[0, rows, :].astype(F32)
-        for b in range(1, 8):
-            total += attn[b, rows, :].astype(F32)
-        write(8 + k, total.astype(BF))
-
-
-def sum_kernel(scal, blocks, total, other):
+def blocks_kernel(x0, y0, x1, y1, x2, y2, attn, out):
+    to = lax.broadcasted_iota(jnp.int32, (HALF, HALF), 0)
+    at = (to % 48 // 12) * 96 + to // 48 * 12 + to % 12
+    pick = (lax.broadcasted_iota(jnp.int32, (HALF, HALF), 1) == at).astype(BF)
+
+    def write(k, rows):
+        out[:, 48 * k : 48 * k + 48, :] = dot(pick, rows).astype(BF).reshape(8, 48, HALF)
+
+    for k, x, y in ((0, x0, y0), (1, x1, y1)):
+        write(k, (x[0].astype(F32) + y[0].astype(F32)).astype(BF))
+    out[:, 144:192, :] = (x2[0].astype(F32) + y2[0].astype(F32)).astype(BF).reshape(8, 48, HALF)
+    total = attn[0].astype(F32)
+    for b in range(1, 8):
+        total += attn[b].astype(F32)
+    write(2, total.astype(BF))
+
+
+def sum_kernel(scal, blocks, mine, other, down):
     core = scal[1]
-    for k in range(15):
-        value = blocks[0, k].astype(F32)
-        for b in range(1, 8):
-            value += blocks[b, k].astype(F32)
-        total[k] = value
-        other[k] = jnp.where(core == 0, value[8:16], value[0:8])
-
-
-def update_kernel(scal, mine, theirs, x_ref, dh1_ref, g1, dres, resid, out_a, out_b, *refs):
+    total = blocks[0].astype(F32)
+    for b in range(1, 8):
+        total += blocks[b].astype(F32)
+    for k in range(12):
+        low, high = total[12 * k : 12 * k + 6, :], total[12 * k + 6 : 12 * k + 12, :]
+        mine[k, 0:6, :] = jnp.where(core == 0, low, high)
+        other[k, 0:6, :] = jnp.where(core == 0, high, low)
+        for out in (mine, other):
+            out[k, 6:8, :] = jnp.zeros((2, HALF), F32)
+    down[...] = total[144:192, :].reshape(3, 16, HALF)
+
+
+def update_kernel(scal, mine, theirs, down, x_ref, dh1_ref, g1, dres, resid, out_a, out_b, *refs):
     core = scal[1]
     output, input_grad = refs[56:58]
     x = x_ref[...].astype(F32)
@@ -599,10 +601,8 @@
         for c in range(0, product.shape[1], 128):
             gain_sums[which] += product[:, c : c + 128]
 
-    own = pl.ds(pl.multiple_of(core * 8, 8), 8)
-
     def chunk(k):
-        a, b = mine[k, own, :][0:6, :], theirs[k][0:6, :]
+        a, b = mine[k][0:6, :], theirs[k][0:6, :]
         return (jnp.where(core == 0, a, b), jnp.where(core == 0, b, a))
 
     for k, weight, offset, gain in (
@@ -626,7 +626,7 @@
                 weigh(gain, weight, at, grad)
     for j in range(3):
         for h in range(2):
-            grad = mine[12 + j, 8 * h : 8 * h + 8, :]
+            grad = down[j, 8 * h : 8 * h + 8, :]
             step(6, (slice(8 * j, 8 * j + 8), slice(h * HALF, (h + 1) * HALF)), grad)
     row = lax.broadcasted_iota(jnp.int32, (6, 128), 0)
     lane = lax.broadcasted_iota(jnp.int32, (6, 128), 1)
@@ -940,18 +940,19 @@
     )(scal, dq, dk, dv, attn, wanted)
     terms, dh1 = reduce_rows(parts, got, dh1)
     dh1 = lax.psum_scatter(dh1, ("z", "core"), scatter_dimension=0, tiled=True)
-    blocks = call(padded_kernel, shape((8, 15, 16, HALF), BF), (*terms, grads), smem=0, name="padded_rows", mib=54)
+    blocks = call(blocks_kernel, shape((8, 192, HALF), BF), (*terms, grads), smem=0, name="own_rows", mib=54)
     blocks = exchange(blocks, 1)
 
-    grads, theirs = call(
-        sum_kernel, (shape((15, 16, HALF), F32), shape((15, 8, HALF), F32)), (scal, blocks), name="sum_blocks", mib=16
+    rows = shape((12, 8, HALF), F32)
+    grads, theirs, down = call(
+        sum_kernel, (rows, rows, shape((3, 16, HALF), F32)), (scal, blocks), name="sum_blocks", mib=16
     )
     theirs = permute(theirs, CORE_PAIRS)
     shapes = tuple(shape(m.shape, F32) for m in masters)
     outs = call(
         update_kernel,
         shapes * 3 + tuple(shape(m.shape, BF) for m in masters) + (shape((128, D), BF), shape((128, D), F32)),
-        (scal, grads, theirs, inputs[0], dh1, g1, dres, resid, out_keep, dh2_other, *masters, *moments, *averages),
+        (scal, grads, theirs, down, inputs[0], dh1, g1, dres, resid, out_keep, dh2_other, *masters, *moments, *averages),
         name="update",
         mib=56,
     )

time: 231 us -> 230 us (level)
    unnamed x40 -> x42, local copies, waits for them, and re-layouts: 7.49 us -> 8.01 us
  transfers between devices with their start and end apart: 24 -> 24, of which waited for: 15 -> 15; matrix products, arithmetic and copies ran while one was open for 5% -> 5% of each run, Pallas kernels for 22% -> 23%
where the time goes in v2:
time: 230 us; the launch traced here: 229 us
  Pallas kernels  83.6 us (36%)
  waiting for transfers between devices  46.4 us (20%)
  starting transfers between devices  46.2 us (20%)
  blocking collectives  17.9 us (8%)
  between operations  14.4 us (6%)
  local copies, waits for them, and re-layouts  11.9 us (5%)
  other arithmetic  9.08 us (4%)
    ppermute x19, waiting for transfers between devices, permute(): return lax.ppermute(value, AXES, pairs)  40.5 us
    pallas_call x9, Pallas kernels, call(): pl.pallas_call(kernel, out_shape=out_shape, in_specs=specs, out_specs=jax...  34.4 us
    ppermute x19, starting transfers between devices, permute(): return lax.ppermute(value, AXES, pairs)  26.4 us
    pallas_call x1, Pallas kernels, shards(): pl.pallas_call(ffn_kernel, out_shape=ffn_out, grid=(4,), in_specs=[scalar...  20 us
    all_to_all x3, starting transfers between devices, exchange(): lax.all_to_all(blocks, AXES, 0, 0, tiled=True, axis_index_groups=cube_gro...  19.7 us
    all_to_all x1, blocking collectives, exchange(): lax.all_to_all(blocks, AXES, 0, 0, tiled=True, axis_index_groups=cube_gro...  17.9 us
    pallas_call x1, Pallas kernels, shards(): pl.pallas_call(attn_backward_kernel, out_shape=(shape((2, 128, D), F32),...  13.8 us
    unnamed x42, local copies, waits for them, and re-layouts  8.01 us
  transfers between devices with their start and end apart: 24, of which 15 were waited for; matrix products, arithmetic and copies ran while one was open for 5% of the time, Pallas kernels for 23%

profile of v2, /device:TPU:1, one launch (start us, length us, event | category | flops | bytes accessed | tf_op | source)
XLA Modules:
  0.0 229.4 jit_solution(7411157510205789100)
XLA Ops:
  7.8 1.6 pack_feed_forward.1
  9.5 1.4 collective-permute-start
  12.7 1.8 merge_feed_forward.1
  16.7 1.5 pack_attention.1
  20.9 1.8 merge_attention.1
  22.7 11.9 %all-to-all-start = ((bf16[8,5,16,384]{3,2,1,0:T(8,128)(2,1)}), bf16[8,5,16,384]{3,2,1,0:T(8,128)(2,1)S(1)}, u32[]{:S(2)}, u32[]{:S(2)}) async-start(bf16[8,5,16,384]{3,2,1,0:T(8,128)(2,1)} %merge_attention.1), calls=%async_computation | async-start | bytes 983040 | tf_op jit(solution)/shard_map/all_to_all | solution.py:85
  36.5 2.4 %all-to-all-done.blocks = bf16[8,5,16,384]{3,2,1,0:T(8,128)(2,1)S(1)} async-done(((bf16[8,5,16,384]{3,2,1,0:T(8,128)(2,1)}), bf16[8,5,16,384]{3,2,1,0:T(8,128)(2,1)S(1)}, u32[]{:S(2)}, u32[]{:S(2)}) %all-to-all-start) | async-done | bytes 491552 | tf_op jit(solution)/shard_map/all_to_all | solution.py:85
  38.9 2.2 dense_rows.1
  41.1 3.6 %all-to-all-start.1 = ((bf16[8,512,384]{2,1,0:T(8,128)(2,1)}), bf16[8,512,384]{2,1,0:T(8,128)(2,1)S(1)}, u32[]{:S(2)}, u32[]{:S(2)}) async-start(bf16[8,512,384]{2,1,0:T(8,128)(2,1)} %dense_rows.1), calls=%async_computation.1 | async-start | bytes 6291456 | tf_op jit(solution)/shard_map/all_to_all | solution.py:85
  44.8 2.4 %collective-permute-start.3 = (bf16[144,768]{1,0:T(8,128)(2,1)S(1)}, bf16[144,768]{1,0:T(8,128)(2,1)S(1)}, u32[]{:S(2)}, u32[]{:S(2)}) collective-permute-start(bf16[144,768]{1,0:T(8,128)(2,1)S(1)} %fusion.2), channel_id=1, source_target_pairs={{0,32},{1,33},{2,34},{3,35},{4,36},{5,37},{6,38},{7,39},{8,40},{9,... | collective-permute-start | bytes 663560 | tf_op jit(solution)/shard_map/ppermute | solution.py:68
  47.9 6.3 %collective-permute-done.3 = bf16[144,768]{1,0:T(8,128)(2,1)S(1)} collective-permute-done((bf16[144,768]{1,0:T(8,128)(2,1)S(1)}, bf16[144,768]{1,0:T(8,128)(2,1)S(1)}, u32[]{:S(2)}, u32[]{:S(2)}) %collective-permute-start.3) | collective-permute-done | bytes 221216 | tf_op jit(solution)/shard_map/ppermute | solution.py:68
  55.1 19.0 %collective-permute-done.4 = bf16[144,768]{1,0:T(8,128)(2,1)S(1)} collective-permute-done((bf16[144,768]{1,0:T(8,128)(2,1)S(1)}, bf16[144,768]{1,0:T(8,128)(2,1)S(1)}, u32[]{:S(2)}, u32[]{:S(2)}) %collective-permute-start.4) | collective-permute-done | bytes 221216 | tf_op jit(solution)/shard_map/ppermute | solution.py:68
  74.1 2.3 collective-permute-done.5
  77.4 1.6 collective-permute-start.6
  82.7 3.1 %fusion = (f32[1024,128]{1,0:T(8,128)}, f32[1024,128]{1,0:T(8,128)}) fusion(f32[128]{0:T(128)S(1)} %mul.184, f32[128]{0:T(128)S(1)} %mul.181, f32[1024]{0:T(1024)S(1)} %get-tuple-element.267), kind=kLoop, calls=%fused_computation.4 | loop fusion | flops 262144 | bytes 1053696 | tf_op jit(solution)/shard_map/mul | solution.py:762
  87.6 16.4 %attention_forward.1 = (bf16[256,384]{1,0:T(8,128)(2,1)}, bf16[1024,384]{1,0:T(8,128)(2,1)}, bf16[1024,384]{1,0:T(8,128)(2,1)}, bf16[1024,768]{1,0:T(8,128)(2,1)...) custom-call(s32[2]{0:T(128)} %pad_add_fusion.1.scal, ...), custom_call_target="tpu_custom_call" | custom-call | flops 13000000512 | bytes 1 | tf_op jit(solution)/shard_map/attention_forward/pallas_call | solution.py:650
  104.3 1.8 collective-permute-done.7.part_b.o_other
  107.0 20.0 %feed_forward.1 = (f32[128,768]{1,0:T(8,128)}, bf16[384,768]{1,0:T(8,128)(2,1)}, f32[256,768]{1,0:T(8,128)}, bf16[4,384,384]{2,1,0:T(8,128)(2,1)}, bf16[4,384,38...) custom-call(s32[2]{0:T(128)} %pad_add_fusion.1.scal, ...), custom_call_target="tpu_custom_call" | custom-call | flops 4001 | bytes 1 | tf_op jit(solution)/shard_map/feed_forward/pallas_call | solution.py:796
  127.4 1.8 collective-permute-done.8.dh2_b.out_b
  131.8 13.8 %attention_backward.1 = (f32[2,128,768]{2,1,0:T(8,128)}, bf16[256,384]{1,0:T(8,128)(2,1)}, bf16[1024,384]{1,0:T(8,128)(2,1)}, bf16[1024,384]{1,0:T(8,128)(2,1)}, bf16[8,384,384]{2,1,0:T(8,128)(2,1)}) custom-call(s32[2]{0:T(128)} %pad_add_fusion.1.scal, f32[256,768]{1,0:T(8,128)} %get-tuple-element.186.resid, bf16[384,768]{1,0:T(8,128)(2,1)} %get-tuple-element.178.dh2_a, ...), custom_call_target="tpu_custom_call" | custom-call | flops 1001 | bytes 1 | tf_op jit(solution)/shard_map/attention_backward/pallas_call | solution.py:848
  148.4 4.7 %next_terms.2 = (bf16[2,384,384]{2,1,0:T(8,128)(2,1)}, bf16[2,384,384]{2,1,0:T(8,128)(2,1)}, bf16[2,384,384]{2,1,0:T(8,128)(2,1)}, bf16[2,384,384]{2,1,0:T(8,128...) custom-call(bf16[4,384,384]{2,1,0:T(8,128)(2,1)} %get-tuple-element.185.refs_0_, ...), custom_call_target="tpu_custom_call" | custom-call | flops 1001 | bytes 1 | tf_op jit(solution)/shard_map/next_terms/pallas_call | solution.py:681
  154.1 4.2 %all-to-all-start.2 = ((bf16[8,384,384]{2,1,0:T(8,128)(2,1)}), bf16[8,384,384]{2,1,0:T(8,128)(2,1)S(1)}, u32[]{:S(2)}, u32[]{:S(2)}) async-start(bf16[8,384,384]{2,1,0:T(8,128)(2,1)} %get-tuple-element.193), calls=%async_computation.2 | async-start | bytes 4718592 | tf_op jit(solution)/shard_map/all_to_all | solution.py:85
  158.3 7.7 %attention_input_gradient.1 = bf16[1024,768]{1,0:T(8,128)(2,1)} custom-call(s32[2]{0:T(128)} %pad_add_fusion.1.scal, bf16[256,384]{1,0:T(8,128)(2,1)} %get-tuple-element.209.dq, bf16[1024,384]{1,0:T(8,128)(2,1)} %get-tuple-element.210.dk, bf16[1024,384]{1,0:T(8,128)(2,1)} %get-tuple-element.211.dv, bf16[8,512,384]{2,1,0:T(8,128)(2,1)} %copy-done.3, ...), custom_call_target="tpu_custom_call" | custom-call | flops 1001 | bytes 1 | tf_op jit(solution)/shard_map/attention_input_gradient/pallas_call | solution.py:923
  167.1 3.0 %next_terms.3 = (bf16[1,384,384]{2,1,0:T(8,128)(2,1)}, bf16[1,384,384]{2,1,0:T(8,128)(2,1)}, bf16[1,384,384]{2,1,0:T(8,128)(2,1)}, bf16[1,384,384]{2,1,0:T(8,128...) custom-call(bf16[2,384,384]{2,1,0:T(8,128)(2,1)} %get-tuple-element.205.refs_0_, ...), custom_call_target="tpu_custom_call" | custom-call | flops 1001 | bytes 1 | tf_op jit(solution)/shard_map/next_terms/pallas_call | solution.py:681
  170.1 1.5 collective-permute-start.15
  174.0 3.4 %all-to-all-done.2.attn = bf16[8,384,384]{2,1,0:T(8,128)(2,1)S(1)} async-done(((bf16[8,384,384]{2,1,0:T(8,128)(2,1)}), bf16[8,384,384]{2,1,0:T(8,128)(2,1)S(1)}, u32[]{:S(2)}, u32[]{:S(2)}) %all-to-all-start.2) | async-done | bytes 2359328 | tf_op jit(solution)/shard_map/all_to_all | solution.py:85
  177.4 2.1 collective-permute-done.15.y0
  179.4 1.7 collective-permute-done.16.y1
  182.0 4.5 %own_rows.1 = bf16[8,192,384]{2,1,0:T(8,128)(2,1)} custom-call(bf16[1,384,384]{2,1,0:T(8,128)(2,1)} %get-tuple-element.217.x0, bf16[1,384,384]{2,1,0:T(8,128)(2,1)} %copy-done.13, bf16[1,384,384]{2,1,0:T(8,128)(2,1)} %get-tuple-element.219.x1, bf16[1,384,384]{2,1,0:T(8,128)(2,1)} %copy-done.14, bf16[1,384,384]{2,1,0:T(8,128)(2,1)} %get-tuple-element.221.x2, ...), custom_call_target="tpu_custom_call" | custom-call | flops 1001 | bytes 1 | tf_op jit(solution)/shard_map/own_rows/pallas_call | solution.py:650
  186.4 17.9 %all_to_all.20.blocks = bf16[8,192,384]{2,1,0:T(8,128)(2,1)S(1)} all-to-all(bf16[8,192,384]{2,1,0:T(8,128)(2,1)} %own_rows.1), channel_id=1, replica_groups={{0,1,4,5,32,33,36,37},{2,3,6,7,34,35,38,39},{8,9,12,13,40,41,44,45},{10..., dimensions={0} | all-to-all | bytes 2359296 | tf_op jit(solution)/shard_map/all_to_all | solution.py:85
  206.4 10.6 %collective-permute-start.18 = (f32[12,8,384]{2,1,0:T(8,128)S(1)}, f32[12,8,384]{2,1,0:T(8,128)S(1)}, u32[]{:S(2)}, u32[]{:S(2)}) collective-permute-start(f32[12,8,384]{2,1,0:T(8,128)S(1)} %get-tuple-element.224), channel_id=1, source_target_pairs={{0,16},{1,17},{2,18},{3,19},{4,20},{5,21},{6,22},{7,23},{8,24},{9,... | collective-permute-start | bytes 442376 | tf_op jit(solution)/shard_map/ppermute | solution.py:68
  218.7 3.8 %update.1 = (f32[6,768]{1,0:T(8,128)}, f32[6,768]{1,0:T(8,128)}, f32[6,768]{1,0:T(8,128)}, f32[6,768]{1,0:T(8,128)}, f32[6,3072]{1,0:T(8,128)}, /*index=5*/f32[6...) custom-call(s32[2]{0:T(128)} %pad_add_fusion.1.scal, ...), custom_call_target="tpu_custom_call" | custom-call | flops 1001 | bytes 1 | tf_op jit(solution)/shard_map/update/pallas_call | solution.py:650
  (114 shorter events, 33.1 us)
Async XLA Ops:
  7.2 99.0 %all-gather.3.cloned.1.call-start = ((), (), s32[]{:S(2)}) async-start(), calls=%async_computation.6 | async-start | bytes 7188480 | tf_op jit(solution)/shard_map/all_gather | solution.py:728
  9.5 2.6 %collective-permute-start = (f32[8,8,384]{2,1,0:T(8,128)}, f32[8,8,384]{2,1,0:T(8,128)S(1)}, u32[]{:S(2)}, u32[]{:S(2)}) collective-permute-start(f32[8,8,384]{2,1,0:T(8,128)} %get-tuple-element.156), channel_id=1, source_target_pairs={{0,16},{1,17},{2,18},{3,19},{4,20},{5,21},{6,22},{7,23},{8,24},{9,... | collective-permute-start | bytes 294920 | tf_op jit(solution)/shard_map/ppermute | solution.py:68
  16.1 4.2 %collective-permute-start.2 = (bf16[128,768]{1,0:T(8,128)(2,1)}, bf16[128,768]{1,0:T(8,128)(2,1)S(1)}, u32[]{:S(2)}, u32[]{:S(2)}) collective-permute-start(bf16[128,768]{1,0:T(8,128)(2,1)} %bitcast.48), channel_id=1, source_target_pairs={{0,16},{1,17},{2,18},{3,19},{4,20},{5,21},{6,22},{7,23},{8,24},{9,... | collective-permute-start | bytes 589832 | tf_op jit(solution)/shard_map/ppermute | solution.py:68
  18.9 1.5 collective-permute-start.1
  20.3 2.4 %copy-start.10 = (bf16[128,768]{1,0:T(8,128)(2,1)}, bf16[128,768]{1,0:T(8,128)(2,1)S(1)}, u32[]{:S(2)}) copy-start(bf16[128,768]{1,0:T(8,128)(2,1)S(1)} %collective-permute-done.2.cot_other) | copy-start | bytes 589828
  22.7 16.2 %all-to-all-start = ((bf16[8,5,16,384]{3,2,1,0:T(8,128)(2,1)}), bf16[8,5,16,384]{3,2,1,0:T(8,128)(2,1)S(1)}, u32[]{:S(2)}, u32[]{:S(2)}) async-start(bf16[8,5,16,384]{3,2,1,0:T(8,128)(2,1)} %merge_attention.1), calls=%async_computation | async-start | bytes 983040 | tf_op jit(solution)/shard_map/all_to_all | solution.py:85
  41.1 44.7 %all-to-all-start.1 = ((bf16[8,512,384]{2,1,0:T(8,128)(2,1)}), bf16[8,512,384]{2,1,0:T(8,128)(2,1)S(1)}, u32[]{:S(2)}, u32[]{:S(2)}) async-start(bf16[8,512,384]{2,1,0:T(8,128)(2,1)} %dense_rows.1), calls=%async_computation.1 | async-start | bytes 6291456 | tf_op jit(solution)/shard_map/all_to_all | solution.py:85
  44.8 34.1 %copy-start.19 = (f32[2]{0:T(128)S(1)}, f32[2]{0:T(128)}, u32[]{:S(2)}) copy-start(f32[2]{0:T(128)} %constant.273.clone) | copy-start | bytes 28
  44.8 9.3 %collective-permute-start.3 = (bf16[144,768]{1,0:T(8,128)(2,1)S(1)}, bf16[144,768]{1,0:T(8,128)(2,1)S(1)}, u32[]{:S(2)}, u32[]{:S(2)}) collective-permute-start(bf16[144,768]{1,0:T(8,128)(2,1)S(1)} %fusion.2), channel_id=1, source_target_pairs={{0,32},{1,33},{2,34},{3,35},{4,36},{5,37},{6,38},{7,39},{8,40},{9,... | collective-permute-start | bytes 663560 | tf_op jit(solution)/shard_map/ppermute | solution.py:68
  47.2 26.9 %collective-permute-start.4 = (bf16[144,768]{1,0:T(8,128)(2,1)S(1)}, bf16[144,768]{1,0:T(8,128)(2,1)S(1)}, u32[]{:S(2)}, u32[]{:S(2)}) collective-permute-start(bf16[144,768]{1,0:T(8,128)(2,1)S(1)} %fusion.2), channel_id=1, source_target_pairs={{0,96},{1,97},{2,98},{3,99},{4,100},{5,101},{6,102},{7,103},{8,104... | collective-permute-start | bytes 663560 | tf_op jit(solution)/shard_map/ppermute | solution.py:68
  54.2 22.2 %collective-permute-start.5 = (bf16[144,768]{1,0:T(8,128)(2,1)S(1)}, bf16[144,768]{1,0:T(8,128)(2,1)S(1)}, u32[]{:S(2)}, u32[]{:S(2)}) collective-permute-start(bf16[144,768]{1,0:T(8,128)(2,1)S(1)} %collective-permute-done.3), channel_id=1, source_target_pairs={{0,96},{1,97},{2,98},{3,99},{4,100},{5,101},{6,102},{7,103},{8,104... | collective-permute-start | bytes 663560 | tf_op jit(solution)/shard_map/ppermute | solution.py:68
  77.4 4.0 %collective-permute-start.6 = (bf16[4,144,768]{2,1,0:T(8,128)(2,1)}, bf16[4,144,768]{2,1,0:T(8,128)(2,1)}, u32[]{:S(2)}, u32[]{:S(2)}) collective-permute-start(bf16[4,144,768]{2,1,0:T(8,128)(2,1)} %pad_maximum_fusion.seq), channel_id=1, source_target_pairs={{0,16},{1,17},{2,18},{3,19},{4,20},{5,21},{6,22},{7,23},{8,24},{9,... | collective-permute-start | bytes 2654216 | tf_op jit(solution)/shard_map/ppermute | solution.py:68
  85.8 1.8 copy-start.3
  104.0 2.2 collective-permute-start.7
  127.0 2.3 %collective-permute-start.8 = (bf16[384,768]{1,0:T(8,128)(2,1)}, bf16[384,768]{1,0:T(8,128)(2,1)S(1)}, u32[]{:S(2)}, u32[]{:S(2)}) collective-permute-start(bf16[384,768]{1,0:T(8,128)(2,1)} %get-tuple-element.178.dh2_a), channel_id=1, source_target_pairs={{0,16},{1,17},{2,18},{3,19},{4,20},{5,21},{6,22},{7,23},{8,24},{9,... | collective-permute-start | bytes 1769480 | tf_op jit(solution)/shard_map/ppermute | solution.py:68
  129.3 2.5 %copy-start.5 = (bf16[384,768]{1,0:T(8,128)(2,1)}, bf16[384,768]{1,0:T(8,128)(2,1)S(1)}, u32[]{:S(2)}) copy-start(bf16[384,768]{1,0:T(8,128)(2,1)S(1)} %collective-permute-done.8.dh2_b.out_b) | copy-start | bytes 1769476
  129.3 16.3 %collective-permute-start.9 = (bf16[4,384,384]{2,1,0:T(8,128)(2,1)}, bf16[4,384,384]{2,1,0:T(8,128)(2,1)S(1)}, u32[]{:S(2)}, u32[]{:S(2)}) collective-permute-start(bf16[4,384,384]{2,1,0:T(8,128)(2,1)} %get-tuple-element.197), channel_id=1, source_target_pairs={{0,3},{1,2},{2,1},{3,0},{4,7},{5,6},{6,5},{7,4},{8,11},{9,10},{10,... | collective-permute-start | bytes 3538952 | tf_op jit(solution)/shard_map/ppermute | solution.py:68
  130.6 15.6 %collective-permute-start.10 = (bf16[4,384,384]{2,1,0:T(8,128)(2,1)}, bf16[4,384,384]{2,1,0:T(8,128)(2,1)S(1)}, u32[]{:S(2)}, u32[]{:S(2)}) collective-permute-start(bf16[4,384,384]{2,1,0:T(8,128)(2,1)} %get-tuple-element.198), channel_id=1, source_target_pairs={{0,12},{1,13},{2,14},{3,15},{4,8},{5,9},{6,10},{7,11},{8,4},{9,5},... | collective-permute-start | bytes 3538952 | tf_op jit(solution)/shard_map/ppermute | solution.py:68
  131.8 15.6 %collective-permute-start.11 = (bf16[4,384,384]{2,1,0:T(8,128)(2,1)}, bf16[4,384,384]{2,1,0:T(8,128)(2,1)S(1)}, u32[]{:S(2)}, u32[]{:S(2)}) collective-permute-start(bf16[4,384,384]{2,1,0:T(8,128)(2,1)} %bitcast.63), channel_id=1, source_target_pairs={{0,96},{1,97},{2,98},{3,99},{4,100},{5,101},{6,102},{7,103},{8,104... | collective-permute-start | bytes 3538952 | tf_op jit(solution)/shard_map/ppermute | solution.py:68
  145.6 1.7 copy-start.7
  153.1 12.9 %collective-permute-start.12 = (bf16[2,384,384]{2,1,0:T(8,128)(2,1)}, bf16[2,384,384]{2,1,0:T(8,128)(2,1)S(1)}, u32[]{:S(2)}, u32[]{:S(2)}) collective-permute-start(bf16[2,384,384]{2,1,0:T(8,128)(2,1)} %get-tuple-element.206), channel_id=1, source_target_pairs={{0,12},{1,13},{2,14},{3,15},{4,8},{5,9},{6,10},{7,11},{8,4},{9,5},... | collective-permute-start | bytes 1769480 | tf_op jit(solution)/shard_map/ppermute | solution.py:68
  153.6 12.5 %collective-permute-start.13 = (bf16[2,384,384]{2,1,0:T(8,128)(2,1)}, bf16[2,384,384]{2,1,0:T(8,128)(2,1)S(1)}, u32[]{:S(2)}, u32[]{:S(2)}) collective-permute-start(bf16[2,384,384]{2,1,0:T(8,128)(2,1)} %get-tuple-element.207), channel_id=1, source_target_pairs={{0,96},{1,97},{2,98},{3,99},{4,100},{5,101},{6,102},{7,103},{8,104... | collective-permute-start | bytes 1769480 | tf_op jit(solution)/shard_map/ppermute | solution.py:68
  153.9 12.1 %collective-permute-start.14 = (bf16[2,384,384]{2,1,0:T(8,128)(2,1)}, bf16[2,384,384]{2,1,0:T(8,128)(2,1)}, u32[]{:S(2)}, u32[]{:S(2)}) collective-permute-start(bf16[2,384,384]{2,1,0:T(8,128)(2,1)} %get-tuple-element.208), channel_id=1, source_target_pairs={{0,3},{1,2},{2,1},{3,0},{4,7},{5,6},{6,5},{7,4},{8,11},{9,10},{10,... | collective-permute-start | bytes 1769480 | tf_op jit(solution)/shard_map/ppermute | solution.py:68
  154.1 23.3 %all-to-all-start.2 = ((bf16[8,384,384]{2,1,0:T(8,128)(2,1)}), bf16[8,384,384]{2,1,0:T(8,128)(2,1)S(1)}, u32[]{:S(2)}, u32[]{:S(2)}) async-start(bf16[8,384,384]{2,1,0:T(8,128)(2,1)} %get-tuple-element.193), calls=%async_computation.2 | async-start | bytes 4718592 | tf_op jit(solution)/shard_map/all_to_all | solution.py:85
  158.3 59.8 %reduce-scatter.2.cloned.1.call-start = ((), (), s32[]{:S(2)}) async-start(), calls=%async_computation.5 | async-start | bytes 1769472 | tf_op jit(solution)/shard_map/reduce_scatter | solution.py:942
  170.1 9.3 %collective-permute-start.15 = (bf16[1,384,384]{2,1,0:T(8,128)(2,1)}, bf16[1,384,384]{2,1,0:T(8,128)(2,1)S(1)}, u32[]{:S(2)}, u32[]{:S(2)}) collective-permute-start(bf16[1,384,384]{2,1,0:T(8,128)(2,1)} %get-tuple-element.218), channel_id=1, source_target_pairs={{0,96},{1,97},{2,98},{3,99},{4,100},{5,101},{6,102},{7,103},{8,104... | collective-permute-start | bytes 884744 | tf_op jit(solution)/shard_map/ppermute | solution.py:68
  171.6 9.6 %collective-permute-start.16 = (bf16[1,384,384]{2,1,0:T(8,128)(2,1)}, bf16[1,384,384]{2,1,0:T(8,128)(2,1)S(1)}, u32[]{:S(2)}, u32[]{:S(2)}) collective-permute-start(bf16[1,384,384]{2,1,0:T(8,128)(2,1)} %get-tuple-element.220), channel_id=1, source_target_pairs={{0,3},{1,2},{2,1},{3,0},{4,7},{5,6},{6,5},{7,4},{8,11},{9,10},{10,... | collective-permute-start | bytes 884744 | tf_op jit(solution)/shard_map/ppermute | solution.py:68
  172.8 8.4 %collective-permute-start.17 = (bf16[1,384,384]{2,1,0:T(8,128)(2,1)}, bf16[1,384,384]{2,1,0:T(8,128)(2,1)S(1)}, u32[]{:S(2)}, u32[]{:S(2)}) collective-permute-start(bf16[1,384,384]{2,1,0:T(8,128)(2,1)} %get-tuple-element.222), channel_id=1, source_target_pairs={{0,12},{1,13},{2,14},{3,15},{4,8},{5,9},{6,10},{7,11},{8,4},{9,5},... | collective-permute-start | bytes 884744 | tf_op jit(solution)/shard_map/ppermute | solution.py:68
  177.4 3.8 %copy-start.4 = (bf16[8,384,384]{2,1,0:T(8,128)(2,1)}, bf16[8,384,384]{2,1,0:T(8,128)(2,1)S(1)}, u32[]{:S(2)}) copy-start(bf16[8,384,384]{2,1,0:T(8,128)(2,1)S(1)} %all-to-all-done.2.attn) | copy-start | bytes 7077892
  179.4 1.7 copy-start.13
  186.4 18.0 %copy-start.2 = (s32[2]{0:T(128)S(1)}, s32[2]{0:T(128)}, u32[]{:S(2)}) copy-start(s32[2]{0:T(128)} %pad_add_fusion.1.scal) | copy-start | bytes 28
  206.4 11.7 %collective-permute-start.18 = (f32[12,8,384]{2,1,0:T(8,128)S(1)}, f32[12,8,384]{2,1,0:T(8,128)S(1)}, u32[]{:S(2)}, u32[]{:S(2)}) collective-permute-start(f32[12,8,384]{2,1,0:T(8,128)S(1)} %get-tuple-element.224), channel_id=1, source_target_pairs={{0,16},{1,17},{2,18},{3,19},{4,20},{5,21},{6,22},{7,23},{8,24},{9,... | collective-permute-start | bytes 442376 | tf_op jit(solution)/shard_map/ppermute | solution.py:68
  (12 other events, 9.7 us)
Sparse Core Ops, SparseCore 0:
  14.7 90.8 all-gather.2
  166.2 50.4 reduce-scatter.1
